TPU v7x, 128 devices: a whole 4x4x4 slice. The times are simulated.
128 devices in a mesh: rep: 16 (over y_hi, x, core), shard: 8 (over z, y_lo).
Axes of the slice: x: 4, y: 4 (y_hi: 2, y_lo: 2; y = y_hi * 2 + y_lo), z: 4, core: 2. Of those that a mesh axis runs over, the one named last changes fastest.
Arguments:
- tokens: bfloat16 [16, 1024, 1024], P('rep', 'shard'), may hold values from -6 to 6
- input_weight: bfloat16 [1024, 3072], P('shard'), may hold values from -0.1875 to 0.1875
- query_value_bias: bfloat16 [2048], P('shard'), may hold values from -3 to 3
- output_weight: bfloat16 [1024, 1024], P('shard'), may hold values from -4 to 4
- output_bias: bfloat16 [1024], P('shard'), may hold values from -3 to 3
- expand_weight: bfloat16 [1024, 4096], P('shard'), may hold values from -0.1875 to 0.1875
- expand_bias: bfloat16 [4096], P('shard'), may hold values from -3 to 3
- reduce_weight: bfloat16 [4096, 1024], P('shard'), may hold values from -0.09375 to 0.09375
- reduce_bias: bfloat16 [1024], P('shard'), may hold values from -3 to 3
- first_gain: bfloat16 [1024], P('shard'), may hold values from 0.5 to 1.5
- first_shift: bfloat16 [1024], P('shard'), may hold values from -3 to 3
- second_gain: bfloat16 [1024], P('shard'), may hold values from 0.5 to 1.5
- second_shift: bfloat16 [1024], P('shard'), may hold values from -3 to 3
- attention_scale: bfloat16 [1024], P('shard'), may hold values from 0.5 to 2
- feedforward_scale: bfloat16 [1024], P('shard'), may hold values from 0.5 to 2
- cotangent: bfloat16 [16, 1024, 1024], P('rep', 'shard'), may hold values from -6 to 6
Outputs:
- layer_output: bfloat16 [16, 1024, 1024], P('rep', 'shard')
- tokens_adjoint: bfloat16 [16, 1024, 1024], P('rep', 'shard')
- input_weight_adjoint: float32 [1024, 3072], P('shard')
- query_value_bias_adjoint: float32 [2048], P('shard')
- output_weight_adjoint: float32 [1024, 1024], P('shard')
- output_bias_adjoint: float32 [1024], P('shard')
- expand_weight_adjoint: float32 [1024, 4096], P('shard')
- expand_bias_adjoint: float32 [4096], P('shard')
- reduce_weight_adjoint: float32 [4096, 1024], P('shard')
- reduce_bias_adjoint: float32 [1024], P('shard')
- first_gain_adjoint: float32 [1024], P('shard')
- first_shift_adjoint: float32 [1024], P('shard')
- second_gain_adjoint: float32 [1024], P('shard')
- second_shift_adjoint: float32 [1024], P('shard')
- attention_scale_adjoint: float32 [1024], P('shard')
- feedforward_scale_adjoint: float32 [1024], P('shard')
All inputs are finite; a program needn't handle non-finite values.
Results may differ from a plain program's by a relative error of at most 0.024.
Values may be sent and summed in bfloat16 or wider, within the bound.
No kernel may reach another device: no remote copies, remote signals or barrier semaphores. Data moves between devices by JAX's collectives and lax.ppermute only.
A program may use at most 128 MiB of HBM per device.

v0:
```python
import jax
import jax.numpy as jnp
from jax import lax
from jax.sharding import PartitionSpec as P

HEAD_DIM = 64


epsilon = 1e-06


def layer_norm(values, gain, shift):
    mean = jnp.mean(values, axis=-1, keepdims=True)
    centred = values - mean
    variance = jnp.mean(centred * centred, axis=-1, keepdims=True)
    return centred * lax.rsqrt(variance + epsilon) * gain + shift


def exact_gelu(values):
    return jax.nn.gelu(values, approximate=False)


def against(left, right):
    return lax.dot_general(
        left, right, (((1,), (1,)), ((), ())), preferred_element_type=jnp.float32
    )


def across(left, right):
    return lax.dot_general(
        left, right, (((0,), (0,)), ((), ())), preferred_element_type=jnp.float32
    )


def attend_forward(query_heads, key_heads, value_heads, scaling):
    scores = (
        jnp.einsum("qhd,khd->hqk", query_heads, key_heads, preferred_element_type=jnp.float32)
        * scaling
    )
    lse = jax.nn.logsumexp(scores, axis=-1, keepdims=True)
    probs = jnp.exp(scores - lse).astype(jnp.bfloat16)
    attended = jnp.einsum("hqk,khd->qhd", probs, value_heads, preferred_element_type=jnp.float32)
    return (attended, lse)


def attend_backward(query_heads, key_heads, value_heads, lse, grad_heads, scaling):
    scores = (
        jnp.einsum("qhd,khd->hqk", query_heads, key_heads, preferred_element_type=jnp.float32)
        * scaling
    )
    weights_full = jnp.exp(scores - lse)
    probs = weights_full.astype(jnp.bfloat16)
    prob_adj = jnp.einsum(
        "qhd,khd->hqk", grad_heads, value_heads, preferred_element_type=jnp.float32
    )
    delta = jnp.sum(weights_full * prob_adj, axis=-1, keepdims=True)
    score_adj = (weights_full * (prob_adj - delta)).astype(jnp.bfloat16)
    return (score_adj, probs)


def by_rows_layer(tokens, params, cotangent):
    f32 = jnp.float32
    bf16 = jnp.bfloat16
    images, rows, width = tokens.shape
    heads = width // HEAD_DIM
    scaling = HEAD_DIM ** (-0.5)
    whole = (
        lax.all_gather(params[0], "shard", axis=0, tiled=True),
        lax.all_gather(params[1], "shard", axis=0, tiled=True),
        lax.all_gather(params[2], "shard", axis=0, tiled=True),
        lax.all_gather(params[3], "shard", axis=0, tiled=True),
        lax.all_gather(params[4], "shard", axis=0, tiled=True),
        lax.all_gather(params[5], "shard", axis=0, tiled=True),
        lax.all_gather(params[6], "shard", axis=0, tiled=True),
        lax.all_gather(params[7], "shard", axis=0, tiled=True),
        lax.all_gather(params[8], "shard", axis=0, tiled=True),
        lax.all_gather(params[9], "shard", axis=0, tiled=True),
        lax.all_gather(params[10], "shard", axis=0, tiled=True),
        lax.all_gather(params[11], "shard", axis=0, tiled=True),
        lax.all_gather(params[12], "shard", axis=0, tiled=True),
        lax.all_gather(params[13], "shard", axis=0, tiled=True),
    )
    in_weight, pair_bias, out_weight, out_bias, up_weight, up_bias = whole[:6]
    down_weight, down_bias = (whole[6], whole[7])
    gain_one, shift_one, gain_two, shift_two, scale_one, scale_two = [
        v.astype(f32) for v in whole[8:]
    ]
    pair_float = pair_bias.astype(f32)
    bias = jnp.concatenate([pair_float[:width], jnp.zeros((width,), f32), pair_float[width:]])
    image = 0
    local = tokens[image].astype(f32)
    hidden = layer_norm(local, gain_one, shift_one).astype(bf16)
    mixed = (jnp.dot(hidden, in_weight, preferred_element_type=f32) + bias).astype(bf16)
    query = mixed[:, :width]
    all_keys = lax.all_gather(mixed[:, width : 2 * width], "shard", axis=0, tiled=True)
    all_values = lax.all_gather(mixed[:, 2 * width :], "shard", axis=0, tiled=True)
    length = all_keys.shape[0]
    query_heads = query.reshape(rows, heads, HEAD_DIM)
    key_heads = all_keys.reshape(length, heads, HEAD_DIM)
    value_heads = all_values.reshape(length, heads, HEAD_DIM)
    attended_f, lse = attend_forward(query_heads, key_heads, value_heads, scaling)
    attended = attended_f.reshape(rows, width).astype(bf16)
    branch = jnp.dot(attended, out_weight, preferred_element_type=f32) + out_bias.astype(f32)
    after = local + scale_one * branch
    second = layer_norm(after, gain_two, shift_two).astype(bf16)
    pre = jnp.dot(second, up_weight, preferred_element_type=f32) + up_bias.astype(f32)
    act = exact_gelu(pre).astype(bf16)
    down = jnp.dot(act, down_weight, preferred_element_type=f32) + down_bias.astype(f32)
    outputs = [(after + scale_two * down).astype(bf16)]
    saved = [
        (
            local,
            hidden,
            query_heads,
            key_heads,
            value_heads,
            lse,
            attended,
            branch,
            after,
            second,
            pre,
            act,
            down,
        )
    ]
    again = (
        lax.all_gather(params[0], "shard", axis=0, tiled=True),
        lax.all_gather(params[1], "shard", axis=0, tiled=True),
        lax.all_gather(params[2], "shard", axis=0, tiled=True),
        lax.all_gather(params[3], "shard", axis=0, tiled=True),
        lax.all_gather(params[4], "shard", axis=0, tiled=True),
        lax.all_gather(params[5], "shard", axis=0, tiled=True),
        lax.all_gather(params[6], "shard", axis=0, tiled=True),
        lax.all_gather(params[7], "shard", axis=0, tiled=True),
        lax.all_gather(params[8], "shard", axis=0, tiled=True),
        lax.all_gather(params[9], "shard", axis=0, tiled=True),
        lax.all_gather(params[10], "shard", axis=0, tiled=True),
        lax.all_gather(params[11], "shard", axis=0, tiled=True),
        lax.all_gather(params[12], "shard", axis=0, tiled=True),
        lax.all_gather(params[13], "shard", axis=0, tiled=True),
    )
    in_weight, out_weight, up_weight, down_weight = (again[0], again[2], again[4], again[6])
    image = 0
    (
        local,
        hidden,
        query_heads,
        key_heads,
        value_heads,
        lse,
        attended,
        branch,
        after,
        second,
        pre,
        act,
        down,
    ) = saved[image]
    upstream = cotangent[image].astype(f32)
    down_adj = (scale_two * upstream).astype(bf16)
    scale_two_adj = jnp.sum(upstream * down, axis=0)
    down_bias_adj = jnp.sum(down_adj.astype(f32), axis=0)
    down_weight_adj = across(act, down_adj)
    act_adj = against(down_adj, down_weight)
    gelu_value, gelu_pull = jax.vjp(exact_gelu, pre)
    pre_adj = gelu_pull(act_adj)[0].astype(bf16)
    up_bias_adj = jnp.sum(pre_adj.astype(f32), axis=0)
    up_weight_adj = across(second, pre_adj)
    second_adj = against(pre_adj, up_weight)
    norm_value, norm_pull = jax.vjp(layer_norm, after, gain_two, shift_two)
    after_inner, gain_two_adj, shift_two_adj = norm_pull(second_adj)
    after_adj = upstream + after_inner
    branch_adj = (scale_one * after_adj).astype(bf16)
    scale_one_adj = jnp.sum(after_adj * branch, axis=0)
    out_bias_adj = jnp.sum(branch_adj.astype(f32), axis=0)
    out_weight_adj = across(attended, branch_adj)
    attended_adj = against(branch_adj, out_weight).astype(bf16)
    grad_heads = attended_adj.reshape(rows, heads, HEAD_DIM)
    score_adj, probs_again = attend_backward(
        query_heads, key_heads, value_heads, lse, grad_heads, scaling
    )
    query_adj = (
        jnp.einsum("hqk,khd->qhd", score_adj, key_heads, preferred_element_type=f32) * scaling
    )
    query_adj = query_adj.reshape(rows, width)
    count = rows * lax.axis_size("shard")
    key_part = (
        jnp.einsum("hqk,qhd->khd", score_adj, query_heads, preferred_element_type=f32) * scaling
    )
    value_part = jnp.einsum("hqk,qhd->khd", probs_again, grad_heads, preferred_element_type=f32)
    pair_adj = lax.psum_scatter(
        jnp.concatenate(
            [key_part.reshape(count, width), value_part.reshape(count, width)], axis=1
        ).astype(jnp.bfloat16),
        "shard",
        scatter_dimension=0,
        tiled=True,
    ).astype(jnp.float32)
    mixed_adj = jnp.concatenate([query_adj, pair_adj], axis=1).astype(bf16)
    column_sums = jnp.sum(mixed_adj.astype(f32), axis=0)
    pair_bias_adj = jnp.concatenate([column_sums[:width], column_sums[2 * width :]])
    in_weight_adj = across(hidden, mixed_adj)
    hidden_adj = against(mixed_adj, in_weight)
    first_value, first_pull = jax.vjp(layer_norm, local, gain_one, shift_one)
    local_inner, gain_one_adj, shift_one_adj = first_pull(hidden_adj)
    adjoints_in = [(after_adj + local_inner).astype(bf16)]
    current = (
        in_weight_adj,
        pair_bias_adj,
        out_weight_adj,
        out_bias_adj,
        up_weight_adj,
        up_bias_adj,
        down_weight_adj,
        down_bias_adj,
        gain_one_adj,
        shift_one_adj,
        gain_two_adj,
        shift_two_adj,
        scale_one_adj,
        scale_two_adj,
    )
    owned = (
        lax.psum_scatter(
            current[0].astype(jnp.bfloat16), "shard", scatter_dimension=0, tiled=True
        ).astype(jnp.float32),
        lax.psum_scatter(
            current[1].astype(jnp.bfloat16), "shard", scatter_dimension=0, tiled=True
        ).astype(jnp.float32),
        lax.psum_scatter(
            current[2].astype(jnp.bfloat16), "shard", scatter_dimension=0, tiled=True
        ).astype(jnp.float32),
        lax.psum_scatter(
            current[3].astype(jnp.bfloat16), "shard", scatter_dimension=0, tiled=True
        ).astype(jnp.float32),
        lax.psum_scatter(
            current[4].astype(jnp.bfloat16), "shard", scatter_dimension=0, tiled=True
        ).astype(jnp.float32),
        lax.psum_scatter(
            current[5].astype(jnp.bfloat16), "shard", scatter_dimension=0, tiled=True
        ).astype(jnp.float32),
        lax.psum_scatter(
            current[6].astype(jnp.bfloat16), "shard", scatter_dimension=0, tiled=True
        ).astype(jnp.float32),
        lax.psum_scatter(
            current[7].astype(jnp.bfloat16), "shard", scatter_dimension=0, tiled=True
        ).astype(jnp.float32),
        lax.psum_scatter(
            current[8].astype(jnp.bfloat16), "shard", scatter_dimension=0, tiled=True
        ).astype(jnp.float32),
        lax.psum_scatter(
            current[9].astype(jnp.bfloat16), "shard", scatter_dimension=0, tiled=True
        ).astype(jnp.float32),
        lax.psum_scatter(
            current[10].astype(jnp.bfloat16), "shard", scatter_dimension=0, tiled=True
        ).astype(jnp.float32),
        lax.psum_scatter(
            current[11].astype(jnp.bfloat16), "shard", scatter_dimension=0, tiled=True
        ).astype(jnp.float32),
        lax.psum_scatter(
            current[12].astype(jnp.bfloat16), "shard", scatter_dimension=0, tiled=True
        ).astype(jnp.float32),
        lax.psum_scatter(
            current[13].astype(jnp.bfloat16), "shard", scatter_dimension=0, tiled=True
        ).astype(jnp.float32),
    )
    return (jnp.stack(outputs), jnp.stack(adjoints_in), owned)


def shards(
    tokens,
    input_weight,
    query_value_bias,
    output_weight,
    output_bias,
    expand_weight,
    expand_bias,
    reduce_weight,
    reduce_bias,
    first_gain,
    first_shift,
    second_gain,
    second_shift,
    attention_scale,
    feedforward_scale,
    cotangent,
):
    params = (
        input_weight,
        query_value_bias,
        output_weight,
        output_bias,
        expand_weight,
        expand_bias,
        reduce_weight,
        reduce_bias,
        first_gain,
        first_shift,
        second_gain,
        second_shift,
        attention_scale,
        feedforward_scale,
    )
    layer_output, tokens_adjoint, owned = by_rows_layer(tokens, params, cotangent)
    final = (
        lax.psum(owned[0].astype(jnp.bfloat16), "rep").astype(jnp.float32),
        lax.psum(owned[1].astype(jnp.bfloat16), "rep").astype(jnp.float32),
        lax.psum(owned[2].astype(jnp.bfloat16), "rep").astype(jnp.float32),
        lax.psum(owned[3].astype(jnp.bfloat16), "rep").astype(jnp.float32),
        lax.psum(owned[4].astype(jnp.bfloat16), "rep").astype(jnp.float32),
        lax.psum(owned[5].astype(jnp.bfloat16), "rep").astype(jnp.float32),
        lax.psum(owned[6].astype(jnp.bfloat16), "rep").astype(jnp.float32),
        lax.psum(owned[7].astype(jnp.bfloat16), "rep").astype(jnp.float32),
        lax.psum(owned[8].astype(jnp.bfloat16), "rep").astype(jnp.float32),
        lax.psum(owned[9].astype(jnp.bfloat16), "rep").astype(jnp.float32),
        lax.psum(owned[10].astype(jnp.bfloat16), "rep").astype(jnp.float32),
        lax.psum(owned[11].astype(jnp.bfloat16), "rep").astype(jnp.float32),
        lax.psum(owned[12].astype(jnp.bfloat16), "rep").astype(jnp.float32),
        lax.psum(owned[13].astype(jnp.bfloat16), "rep").astype(jnp.float32),
    )
    return (
        layer_output,
        tokens_adjoint,
        final[0],
        final[1],
        final[2],
        final[3],
        final[4],
        final[5],
        final[6],
        final[7],
        final[8],
        final[9],
        final[10],
        final[11],
        final[12],
        final[13],
    )


def solution(mesh):
    placed = (
        P("rep", "shard", None),
        P("shard", None),
        P("shard"),
        P("shard", None),
        P("shard"),
        P("shard", None),
        P("shard"),
        P("shard", None),
        P("shard"),
        P("shard"),
        P("shard"),
        P("shard"),
        P("shard"),
        P("shard"),
        P("shard"),
        P("rep", "shard", None),
    )
    return jax.shard_map(
        shards,
        mesh=mesh,
        in_specs=placed,
        out_specs=(
            P("rep", "shard", None),
            P("rep", "shard", None),
            P("shard", None),
            P("shard"),
            P("shard", None),
            P("shard"),
            P("shard", None),
            P("shard"),
            P("shard", None),
            P("shard"),
            P("shard"),
            P("shard"),
            P("shard"),
            P("shard"),
            P("shard"),
            P("shard"),
        ),
        check_vma=False,
    )
```

profile of v0, /device:TPU:1, one launch (start us, length us, event | category | flops | bytes accessed | tf_op | source)
XLA Modules:
  0.0 1479.9 jit_solution(1282801195547439109)
XLA Ops:
  7.2 0.7 all-gather.17.cloned.1.call-update
  8.0 0.7 reshape.162
  8.6 17.3 %all-gather.1 = bf16[8,1,128]{2,1,0:T(2,128)(2,1)S(1)} all-gather(bf16[1,1,128]{2,1,0:T(2,128)(2,1)} %bitcast.165), channel_id=1, replica_groups=mesh['rep'=16,'shard'=8] {'shard'}, dimensions={0}, use_global_device_ids=true | all-gather | bytes 2304 | tf_op jit(solution)/shard_map/all_gather | solution.py:76
  25.9 12.6 all-gather.2
  38.4 14.6 all-gather.3
  53.1 1.1 convert_reduce_fusion
  54.2 1.2 fusion.22
  55.3 87.2 %all-gather.17.cloned.1.call-done = bf16[1024,3072]{1,0:T(8,128)(2,1)} async-done(((bf16[128,3072]{1,0:T(8,128)(2,1)}), bf16[1024,3072]{1,0:T(8,128)(2,1)}) %all-gather.17.cloned.1.call-update) | async-done | bytes 6291472 | tf_op jit(solution)/shard_map/all_gather | solution.py:68
  142.5 4.0 fusion.1
  146.6 0.8 fusion.50
  147.5 0.7 all-gather.19.cloned.1.call-update
  150.0 14.0 all-gather.4
  164.0 12.6 all-gather.6
  176.5 14.3 all-gather.7
  190.9 12.2 all-gather
  203.1 13.3 all-gather.5
  216.4 21.5 %all-gather.8 = bf16[8,1,512]{2,1,0:T(2,128)(2,1)S(1)} all-gather(bf16[1,1,512]{2,1,0:T(2,128)(2,1)S(1)} %reshape.172), channel_id=1, replica_groups=mesh['rep'=16,'shard'=8] {'shard'}, dimensions={0}, use_global_device_ids=true | all-gather | bytes 9216 | tf_op jit(solution)/shard_map/all_gather | solution.py:73
  238.1 2.9 copy.46
  241.1 13.6 all-gather.19.cloned.1.call-done
  254.6 3.9 copy.44
  258.6 1.4 multiply_reduce_fusion.1
  260.0 1.8 exponential_reduce_fusion
  261.8 1.7 copy-done
  263.5 1.9 convolution_convert_fusion.6
  265.5 42.1 %all-gather.23.cloned.1.call-done = bf16[1024,1024]{1,0:T(8,128)(2,1)} async-done(((bf16[128,1024]{1,0:T(8,128)(2,1)}), bf16[1024,1024]{1,0:T(8,128)(2,1)}) %all-gather.23.cloned.1.call-update) | async-done | bytes 2097168 | tf_op jit(solution)/shard_map/all_gather | solution.py:70
  307.6 2.9 fusion.48
  310.7 166.1 %all-gather.25.cloned.1.call-done = bf16[1024,4096]{1,0:T(8,128)(2,1)} async-done(((bf16[128,4096]{1,0:T(8,128)(2,1)}), bf16[1024,4096]{1,0:T(8,128)(2,1)}) %all-gather.25.cloned.1.call-update) | async-done | bytes 8388624 | tf_op jit(solution)/shard_map/all_gather | solution.py:72
  476.8 9.3 multiply_convert_fusion.2
  486.1 161.6 %all-gather.27.cloned.1.call-done = bf16[4096,1024]{1,0:T(8,128)(2,1)} async-done(((bf16[512,1024]{1,0:T(8,128)(2,1)}), bf16[4096,1024]{1,0:T(8,128)(2,1)}) %all-gather.27.cloned.1.call-update) | async-done | bytes 8388624 | tf_op jit(solution)/shard_map/all_gather | solution.py:74
  647.7 10.1 fusion.53
  657.9 3.0 multiply_reduce_fusion.3
  661.4 0.7 copy-done.16
  662.6 1.5 convolution_convert_fusion.5
  664.1 1.8 copy.47
  665.9 5.5 convolution_convert_fusion.3
  671.4 5.3 multiply_reduce_fusion
  676.8 2.0 multiply_convert_fusion
  678.8 0.7 multiply_convert_fusion.1
  679.5 1.2 copy-done.1
  680.8 2.4 pad_maximum_fusion
  683.2 6.5 copy.48
  689.8 3.0 convolution_convert_fusion.4
  692.9 6.9 convolution_convert_fusion.1
  700.1 6.9 convolution_convert_fusion
  707.1 4.4 fusion.8
  711.5 70.7 %reduce-scatter.16.cloned.1.call-done = bf16[128,2048]{1,0:T(8,128)(2,1)} async-done(((bf16[1024,2048]{1,0:T(8,128)(2,1)}), bf16[128,2048]{1,0:T(8,128)(2,1)}) %reduce-scatter.16.cloned.1.call-update) | async-done | bytes 524304
  782.2 1.3 copy.49
  783.6 5.6 convolution_convert_fusion.2
  789.3 48.5 %reduce-scatter.10.cloned.1.call-done = bf16[128,1024]{1,0:T(8,128)(2,1)} async-done(((bf16[1024,1024]{1,0:T(8,128)(2,1)}), bf16[128,1024]{1,0:T(8,128)(2,1)}) %reduce-scatter.10.cloned.1.call-update) | async-done | bytes 262160 | tf_op jit(solution)/shard_map/reduce_scatter | solution.py:231
  837.7 170.9 %reduce-scatter.12.cloned.1.call-done = bf16[128,4096]{1,0:T(8,128)(2,1)} async-done(((bf16[1024,4096]{1,0:T(8,128)(2,1)}), bf16[128,4096]{1,0:T(8,128)(2,1)}) %reduce-scatter.12.cloned.1.call-update) | async-done | bytes 1048592 | tf_op jit(solution)/shard_map/reduce_scatter | solution.py:237
  1008.7 172.5 %reduce-scatter.14.cloned.1.call-done = bf16[512,1024]{1,0:T(8,128)(2,1)} async-done(((bf16[4096,1024]{1,0:T(8,128)(2,1)}), bf16[512,1024]{1,0:T(8,128)(2,1)}) %reduce-scatter.14.cloned.1.call-update) | async-done | bytes 1048592 | tf_op jit(solution)/shard_map/reduce_scatter | solution.py:243
  1181.1 133.5 %reduce-scatter.8.cloned.1.call-done = bf16[128,3072]{1,0:T(8,128)(2,1)} async-done(((bf16[1024,3072]{1,0:T(8,128)(2,1)}), bf16[128,3072]{1,0:T(8,128)(2,1)}) %reduce-scatter.8.cloned.1.call-update) | async-done | bytes 786448 | tf_op jit(solution)/shard_map/reduce_scatter | solution.py:225
  1314.7 0.6 dynamic-slice
  1317.2 13.2 all-gather.9
  1330.7 5.2 fusion.45
  1336.4 5.8 fusion.25
  1342.2 25.6 %all-reduce.12 = (bf16[2048]{0:T(1024)(128)(2,1)S(1)}, bf16[1024]{0:T(1024)(128)(2,1)S(1)}, bf16[4096]{0:T(1024)(128)(2,1)S(1)}, bf16[1024]{0:T(1024)(128)(2,1)S...) all-reduce(bf16[2048]{0:T(1024)(128)(2,1)S(1)} %pad_maximum_fusion., ...), channel_id=4, replica_groups=mesh['rep'=16,'shard'=8] {'shard'}, use_global_device_ids=true, to_apply=%region_15.0.clone | all-reduce | flops 14336 | bytes 57344
  1368.5 43.8 %all-reduce.10 = (bf16[256]{0:T(256)(128)(2,1)S(1)}, bf16[128]{0:T(256)(128)(2,1)S(1)}, bf16[512]{0:T(512)(128)(2,1)S(1)}, bf16[128]{0:T(256)(128)(2,1)S(1)}, bf...) all-reduce(bf16[256]{0:T(256)(128)(2,1)S(1)} %dynamic-slice.1, ...), channel_id=1, replica_groups=mesh['rep'=16,'shard'=8] {'rep'}, use_global_device_ids=true, to_apply=%region_16.0 | all-reduce | flops 1792 | bytes 7168 | tf_op jit(solution)/shard_map/psum | solution.py:308
  1417.0 0.6 convert_element_type.239
  1417.5 47.7 %all-reduce.15.cloned.1.call-done = (bf16[128,3072]{1,0:T(8,128)(2,1)}, bf16[128,1024]{1,0:T(8,128)(2,1)}, bf16[128,4096]{1,0:T(8,128)(2,1)}, bf16[512,1024]{1,0:T(8,128)(2,1)}) async-done(((bf16[128,3072]{1,0:T(8,128)(2,1)}, bf16[128,1024]{1,0:T(8,128)(2,1)}, bf16[128,4096]{1,0:T(8,128)(2,1)}, bf16[512,1024]{1,0:T(8,128)(2,1)}), (bf16[128,3072]{1,0:T(8,128)(2,1)}, bf16[128,1024]{1,0:T(8,128)(2,1)}, ...) | async-done | bytes 3145744 | tf_op jit(solution)/shard_map/psum | solution.py:307
  1465.2 1.9 convert_element_type.235
  1467.1 2.4 convert_element_type.231
  1469.5 1.5 convert_element_type.238
  1471.1 1.6 convert_element_type.241
  (133 shorter events, 10.1 us)
Async XLA Ops:
  7.2 135.3 %all-gather.17.cloned.1.call-start = ((), (), s32[]{:S(2)}) async-start(), calls=%async_computation.5 | async-start | bytes 7077888 | tf_op jit(solution)/shard_map/all_gather | solution.py:68
  7.9 230.2 %all-gather.21.cloned.1.call-start = ((), (), s32[]{:S(2)}) async-start(), calls=%async_computation.7 | async-start | bytes 2359296 | tf_op jit(solution)/shard_map/all_gather | solution.py:95
  146.5 3.5 copy-start.21
  146.5 3.5 copy-start.22
  146.5 17.4 %copy-start.23 = (bf16[128]{0:T(256)(128)(2,1)S(1)}, bf16[128]{0:T(256)(128)(2,1)}, u32[]{:S(2)}) copy-start(bf16[128]{0:T(256)(128)(2,1)} %param.27) | copy-start | bytes 772
  146.5 30.0 %copy-start.24 = (bf16[128]{0:T(256)(128)(2,1)S(1)}, bf16[128]{0:T(256)(128)(2,1)}, u32[]{:S(2)}) copy-start(bf16[128]{0:T(256)(128)(2,1)} %param.28) | copy-start | bytes 772
  146.5 44.3 %copy-start.25 = (bf16[128]{0:T(256)(128)(2,1)S(1)}, bf16[128]{0:T(256)(128)(2,1)}, u32[]{:S(2)}) copy-start(bf16[128]{0:T(256)(128)(2,1)} %param.29) | copy-start | bytes 772
  146.5 56.5 %copy-start.26 = (bf16[128]{0:T(256)(128)(2,1)S(1)}, bf16[128]{0:T(256)(128)(2,1)}, u32[]{:S(2)}) copy-start(bf16[128]{0:T(256)(128)(2,1)} %param.30) | copy-start | bytes 772
  147.4 107.2 %all-gather.19.cloned.1.call-start = ((), (), s32[]{:S(2)}) async-start(), calls=%async_computation.6 | async-start | bytes 2359296 | tf_op jit(solution)/shard_map/all_gather | solution.py:96
  148.2 159.5 %all-gather.23.cloned.1.call-start = ((), (), s32[]{:S(2)}) async-start(), calls=%async_computation.8 | async-start | bytes 2359296 | tf_op jit(solution)/shard_map/all_gather | solution.py:70
  148.7 328.0 %all-gather.25.cloned.1.call-start = ((), (), s32[]{:S(2)}) async-start(), calls=%async_computation.9 | async-start | bytes 9437184 | tf_op jit(solution)/shard_map/all_gather | solution.py:72
  149.3 498.4 %all-gather.27.cloned.1.call-start = ((), (), s32[]{:S(2)}) async-start(), calls=%async_computation.10 | async-start | bytes 9437184 | tf_op jit(solution)/shard_map/all_gather | solution.py:74
  149.9 632.3 %reduce-scatter.16.cloned.1.call-start = ((), (), s32[]{:S(2)}) async-start(), calls=%async_computation.15 | async-start | bytes 4718592
  238.1 20.5 %copy-start.14 = (bf16[128,1024]{0,1:T(8,128)(2,1)}, bf16[128,1024]{0,1:T(8,128)(2,1)S(1)}, u32[]{:S(2)}) copy-start(bf16[128,1024]{0,1:T(8,128)(2,1)S(1)} %copy.45) | copy-start | bytes 786436
  259.9 3.6 copy-start
  260.0 3.5 copy-start.2
  263.5 44.1 %copy-start.4 = (bf16[1,128,1024]{2,1,0:T(8,128)(2,1)S(1)}, bf16[1,128,1024]{2,1,0:T(8,128)(2,1)}, u32[]{:S(2)}) copy-start(bf16[1,128,1024]{2,1,0:T(8,128)(2,1)} %param.16) | copy-start | bytes 786436
  265.4 45.2 %copy-start.17 = (bf16[16,64,128]{2,1,0:T(8,128)(2,1)}, bf16[16,64,128]{2,1,0:T(8,128)(2,1)S(1)}, u32[]{:S(2)}) copy-start(bf16[16,64,128]{2,1,0:T(8,128)(2,1)S(1)} %convolution_convert_fusion.6) | copy-start | bytes 786436
  476.8 170.9 %copy-start.9 = (bf16[1,128,1024]{2,1,0:T(8,128)(2,1)S(1)}, bf16[1,128,1024]{2,1,0:T(8,128)(2,1)}, u32[]{:S(2)}) copy-start(bf16[1,128,1024]{2,1,0:T(8,128)(2,1)} %param.31) | copy-start | bytes 786436
  647.7 10.2 copy-start.6
  657.9 3.1 copy-start.8
  657.9 3.3 copy-start.10
  660.9 1.7 copy-start.7
  661.4 0.7 copy-start.16
  665.9 5.5 copy-start.3
  665.9 5.5 copy-start.12
  665.9 10.8 slice-start
  671.4 5.3 slice-start.1
  676.7 2.1 copy-start.15
  678.8 2.0 copy-start.1
  689.7 148.0 %reduce-scatter.10.cloned.1.call-start = ((), (), s32[]{:S(2)}) async-start(), calls=%async_computation.12 | async-start | bytes 2359296 | tf_op jit(solution)/shard_map/reduce_scatter | solution.py:231
  692.9 315.8 %reduce-scatter.12.cloned.1.call-start = ((), (), s32[]{:S(2)}) async-start(), calls=%async_computation.13 | async-start | bytes 9437184 | tf_op jit(solution)/shard_map/reduce_scatter | solution.py:237
  699.8 481.3 %reduce-scatter.14.cloned.1.call-start = ((), (), s32[]{:S(2)}) async-start(), calls=%async_computation.14 | async-start | bytes 9437184 | tf_op jit(solution)/shard_map/reduce_scatter | solution.py:243
  707.0 607.6 %reduce-scatter.8.cloned.1.call-start = ((), (), s32[]{:S(2)}) async-start(), calls=%async_computation.11 | async-start | bytes 7077888 | tf_op jit(solution)/shard_map/reduce_scatter | solution.py:225
  789.2 525.5 %copy-start.28 = (u32[128]{0:T(128)S(1)}, u32[128]{0:T(128)}, u32[]{:S(2)}) copy-start(u32[128]{0:T(128)} %constant.95) | copy-start | bytes 1540
  789.2 528.0 %copy-start.27 = (bf16[128]{0:T(256)(128)(2,1)S(1)}, bf16[128]{0:T(256)(128)(2,1)}, u32[]{:S(2)}) copy-start(bf16[128]{0:T(256)(128)(2,1)} %param.24) | copy-start | bytes 772
  789.2 541.2 %copy-start.13 = (bf16[16,64,128]{2,1,0:T(8,128)(2,1)S(1)}, bf16[16,64,128]{2,1,0:T(8,128)(2,1)}, u32[]{:S(2)}) copy-start(bf16[16,64,128]{2,1,0:T(8,128)(2,1)} %fusion.8) | copy-start | bytes 786436
  789.2 676.0 %all-reduce.15.cloned.1.call-start = ((), (), s32[]{:S(2)}) async-start(), calls=%async_computation.16 | async-start | bytes 6291456 | tf_op jit(solution)/shard_map/psum | solution.py:307
  1330.7 5.6 copy-start.5
  1330.7 5.6 copy-start.11
  1330.7 5.6 copy-start.18
  1465.2 4.3 copy-start.20
  1469.5 1.5 copy-start.19
Sparse Core Ops, SparseCore 0:
  9.7 132.8 all-gather.16
  147.5 53.0 all-gather.20
  202.8 51.7 all-gather.18
  256.1 51.4 all-gather.22
  309.1 167.6 all-gather.24
  478.3 169.3 all-gather.26
  689.9 92.3 reduce-scatter.15
  785.2 52.4 reduce-scatter.9
  840.1 168.4 reduce-scatter.11
  1010.9 170.1 reduce-scatter.13
  1183.6 131.0 reduce-scatter.7
  1317.3 147.9 all-reduce.14
where the time goes:
time: 1480 us
  waiting for transfers between devices  1120 us (76%)
  blocking collectives  215 us (15%)
  matrix products  83.5 us (6%)
  local copies, waits for them, and re-layouts  23.8 us (2%)
  other arithmetic  22.6 us (2%)
  between operations  17.2 us (1%)
    reduce_scatter x1, waiting for transfers between devices, by_rows_layer(): lax.psum_scatter(current[6].astype(jnp.bfloat16), 'shard', scatter_dimens...  172 us
    reduce_scatter x1, waiting for transfers between devices, by_rows_layer(): lax.psum_scatter(current[4].astype(jnp.bfloat16), 'shard', scatter_dimens...  171 us
    all_gather x1, waiting for transfers between devices, by_rows_layer(): lax.all_gather(params[4], 'shard', axis=0, tiled=True)  166 us
    all_gather x1, waiting for transfers between devices, by_rows_layer(): lax.all_gather(params[6], 'shard', axis=0, tiled=True)  162 us
    reduce_scatter x1, waiting for transfers between devices, by_rows_layer(): lax.psum_scatter(current[0].astype(jnp.bfloat16), 'shard', scatter_dimens...  133 us
    all_gather x1, waiting for transfers between devices, by_rows_layer(): lax.all_gather(params[0], 'shard', axis=0, tiled=True)  87.2 us
    unnamed x13, waiting for transfers between devices  73.8 us
    reduce_scatter x1, waiting for transfers between devices, by_rows_layer(): lax.psum_scatter(current[2].astype(jnp.bfloat16), 'shard', scatter_dimens...  48.5 us
  transfers between devices with their start and end apart: 12, of which 11 were waited for; matrix products, arithmetic and copies ran while one was open for 5% of the time, Pallas kernels for 0%

commit v1 on v0

v1 whole, which is shorter than its diff:
```python
import jax
import jax.numpy as jnp
from jax import lax
from jax.sharding import Mesh, PartitionSpec as P

HEAD_DIM = 64
EPSILON = 1e-06
SHARD = ("z", "yl")
REP = ("yh", "x", "core")
NZ, NX = 4, 4
f32 = jnp.float32
bf16 = jnp.bfloat16


def normalised(values):
    mean = jnp.mean(values, axis=-1, keepdims=True)
    centred = values - mean
    variance = jnp.mean(centred * centred, axis=-1, keepdims=True)
    return centred * lax.rsqrt(variance + EPSILON)


def layer_norm(values, gain, shift):
    return normalised(values) * gain + shift


def exact_gelu(values):
    return jax.nn.gelu(values, approximate=False)


def times(left, right):
    return jnp.dot(left, right, preferred_element_type=f32)


def against(left, right):
    return lax.dot_general(left, right, (((1,), (1,)), ((), ())), preferred_element_type=f32)


def across(left, right):
    return lax.dot_general(left, right, (((0,), (0,)), ((), ())), preferred_element_type=f32)


SWAP = [(0, 1), (1, 0)]


def from_ahead(block, axis, n, k):
    return lax.ppermute(block, axis, [((i + k) % n, i) for i in range(n)])


def to_ahead(block, axis, n, k):
    return lax.ppermute(block, axis, [(i, (i + k) % n) for i in range(n)])


def gather_shard(block):
    other = lax.ppermute(block, "yl", SWAP)
    near = [block] + [from_ahead(block, "z", NZ, k) for k in range(1, NZ)]
    far = [other] + [from_ahead(other, "z", NZ, k) for k in range(1, NZ)]
    return near + far


def scatter_sum_shard(parts, rows):
    def along_z(base):
        total = parts[base * rows : (base + 1) * rows].astype(f32)
        for k in range(1, NZ):
            sent = parts[(base + k) * rows : (base + k + 1) * rows]
            total = total + to_ahead(sent, "z", NZ, k).astype(f32)
        return total

    other = lax.ppermute(along_z(NZ).astype(bf16), "yl", SWAP)
    return along_z(0) + other.astype(f32)


def pick(array, index, axis=0):
    return lax.dynamic_index_in_dim(array, index, axis, keepdims=False)


def reduce_rep(parts, core, x):
    parts = parts.astype(bf16)
    mine = pick(parts, core).astype(f32)
    total = (mine + lax.ppermute(pick(parts, 1 - core), "core", SWAP).astype(f32)).astype(bf16)
    mine = pick(total, x).astype(f32)
    for k in range(1, NX):
        mine = mine + to_ahead(pick(total, (x + k) % NX), "x", NX, k).astype(f32)
    mine = mine.astype(bf16)
    other = lax.ppermute(mine, "yh", SWAP)
    return (mine.astype(f32) + other.astype(f32)).astype(bf16)


def spread_rep(block):
    return lax.all_gather(block, ("core", "x"), axis=0, tiled=True)


def attend_forward(query, key, value, scaling):
    scores = jnp.einsum("qhd,khd->hqk", query, key, preferred_element_type=f32) * scaling
    lse = jax.nn.logsumexp(scores, axis=-1, keepdims=True)
    probs = jnp.exp(scores - lse).astype(bf16)
    attended = jnp.einsum("hqk,khd->qhd", probs, value, preferred_element_type=f32)
    return attended, lse


def attend_backward(query, key, value, lse, grad, scaling):
    scores = jnp.einsum("qhd,khd->hqk", query, key, preferred_element_type=f32) * scaling
    weights = jnp.exp(scores - lse)
    probs = weights.astype(bf16)
    prob_adj = jnp.einsum("qhd,khd->hqk", grad, value, preferred_element_type=f32)
    delta = jnp.sum(weights * prob_adj, axis=-1, keepdims=True)
    score_adj = (weights * (prob_adj - delta)).astype(bf16)
    query_adj = jnp.einsum("hqk,khd->qhd", score_adj, key, preferred_element_type=f32) * scaling
    key_adj = jnp.einsum("hqk,qhd->khd", score_adj, query, preferred_element_type=f32) * scaling
    value_adj = jnp.einsum("hqk,qhd->khd", probs, grad, preferred_element_type=f32)
    return query_adj, key_adj, value_adj


def shards(
    tokens,
    input_weight,
    query_value_bias,
    output_weight,
    output_bias,
    expand_weight,
    expand_bias,
    reduce_weight,
    reduce_bias,
    first_gain,
    first_shift,
    second_gain,
    second_shift,
    attention_scale,
    feedforward_scale,
    cotangent,
):
    _, rows, width = tokens.shape
    units = reduce_weight.shape[0]
    part = output_weight.shape[0]
    heads = part // HEAD_DIM
    group = 8
    length = group * rows
    scaling = HEAD_DIM ** (-0.5)
    z, yl = lax.axis_index("z"), lax.axis_index("yl")
    x, core = lax.axis_index("x"), lax.axis_index("core")
    me = z * 2 + yl

    w = input_weight.reshape(part, 3, group, part)
    in_w = lax.all_to_all(w, SHARD, split_axis=2, concat_axis=0, tiled=True).reshape(width, 3 * part)
    w = expand_weight.reshape(part, group, units)
    up_w = lax.all_to_all(w, SHARD, split_axis=1, concat_axis=0, tiled=True).reshape(width, units)

    small = jnp.concatenate(
        [
            query_value_bias,
            output_bias,
            reduce_bias,
            first_gain,
            first_shift,
            second_gain,
            second_shift,
            attention_scale,
            feedforward_scale,
        ]
    )
    extra = 8
    small = jnp.pad(small, (0, extra * width - small.shape[0])).reshape(extra, width)
    own = tokens[0]
    blocks = gather_shard(jnp.concatenate([own, small], axis=0))
    all_tokens = jnp.concatenate([b[:rows] for b in blocks], axis=0).astype(f32)
    smalls = jnp.stack([b[rows : rows + 2].reshape(2 * width) for b in blocks])
    zz, yy = jnp.arange(group) // 2, jnp.arange(group) % 2
    place = ((yy - yl) % 2) * NZ + (zz - z) % NZ
    chosen = (place[:, None] == jnp.arange(group)[None, :]).astype(bf16)
    smalls = times(chosen, smalls)
    pair_bias = smalls[:, : 2 * part].reshape(2 * width)
    out_bias, down_bias, gain_one, shift_one, gain_two, shift_two, scale_one, scale_two = [
        smalls[:, (2 + j) * part : (3 + j) * part].reshape(width) for j in range(8)
    ]
    bias = jnp.concatenate(
        [
            lax.dynamic_slice(pair_bias, (me * part,), (part,)),
            jnp.zeros((part,), f32),
            lax.dynamic_slice(pair_bias, (width + me * part,), (part,)),
        ]
    )
    upstreams = jnp.concatenate(gather_shard(cotangent[0]), axis=0).astype(f32)

    local = own.astype(f32)
    normal_one = normalised(all_tokens)
    hidden = (normal_one * gain_one + shift_one).astype(bf16)
    mixed = (times(hidden, in_w) + bias).astype(bf16)
    query, key, value = [
        mixed[:, j * part : (j + 1) * part].reshape(length, heads, HEAD_DIM) for j in range(3)
    ]
    attended, lse = attend_forward(query, key, value, scaling)
    attended = attended.reshape(length, part).astype(bf16)
    branch = scatter_sum_shard(times(attended, output_weight).astype(bf16), rows) + out_bias
    after = local + scale_one * branch

    second_own = layer_norm(after, gain_two, shift_two).astype(bf16)
    second = jnp.concatenate(gather_shard(second_own), axis=0)
    pre = times(second, up_w) + expand_bias.astype(f32)
    act = exact_gelu(pre).astype(bf16)

    down_adj = (scale_two * upstreams).astype(bf16)
    act_adj = against(down_adj, reduce_weight)
    _, gelu_pull = jax.vjp(exact_gelu, pre)
    pre_adj = gelu_pull(act_adj)[0].astype(bf16)
    second_adj = scatter_sum_shard(against(pre_adj, up_w).astype(bf16), rows)
    up_bias_adj = jnp.sum(pre_adj.astype(f32), axis=0)
    down_weight_adj = across(act, down_adj)
    up_weight_adj = across(second, pre_adj)

    upstream = cotangent[0].astype(f32)
    _, norm_pull = jax.vjp(layer_norm, after, gain_two, shift_two)
    after_inner, gain_two_adj, shift_two_adj = norm_pull(second_adj)
    after_adj = upstream + after_inner
    branch_adj_own = (scale_one * after_adj).astype(bf16)
    scale_one_adj = jnp.sum(after_adj * branch, axis=0)
    out_bias_adj = jnp.sum(branch_adj_own.astype(f32), axis=0)
    branch_adj = jnp.concatenate(gather_shard(branch_adj_own), axis=0)

    down = scatter_sum_shard(times(act, reduce_weight).astype(bf16), rows) + down_bias
    layer_output = (after + scale_two * down).astype(bf16)
    scale_two_adj = jnp.sum(upstream * down, axis=0)
    down_bias_adj = jnp.sum((scale_two * upstream).astype(bf16).astype(f32), axis=0)

    attended_adj = against(branch_adj, output_weight).astype(bf16)
    out_weight_adj = across(attended, branch_adj)
    grad = attended_adj.reshape(length, heads, HEAD_DIM)
    pieces = attend_backward(query, key, value, lse, grad, scaling)
    mixed_adj = jnp.concatenate([p.reshape(length, part) for p in pieces], axis=1).astype(bf16)
    hidden_part = against(mixed_adj, in_w)
    hidden_adj = scatter_sum_shard(hidden_part.astype(bf16), rows)
    _, first_pull = jax.vjp(lambda v: normalised(v) * gain_one, local)
    tokens_adjoint = (after_adj + first_pull(hidden_adj)[0]).astype(bf16)
    gain_one_adj = jnp.sum(hidden_part * normal_one, axis=0)
    shift_one_adj = jnp.sum(hidden_part, axis=0)
    in_weight_adj = across(hidden, mixed_adj)
    sums = jnp.sum(mixed_adj.astype(f32), axis=0)

    piece = part // 8

    def by_rows(array, kinds):
        columns = array.shape[-1]
        array = array.reshape(group, 2, NX, piece, columns)
        array = reduce_rep(array.transpose(1, 2, 0, 3, 4), core, x)
        array = lax.all_to_all(array, SHARD, split_axis=0, concat_axis=0, tiled=True)
        array = array.reshape(group, piece, kinds, columns // kinds).transpose(1, 2, 0, 3)
        array = array.reshape(piece, group * columns)
        return spread_rep(array).astype(f32)

    def in_place(array):
        n, columns = array.shape
        array = reduce_rep(array.reshape(2, NX, n // 8, columns), core, x)
        return spread_rep(array).astype(f32)

    down_weight_adj = in_place(down_weight_adj)
    up_weight_adj = by_rows(up_weight_adj, 1)
    out_weight_adj = in_place(out_weight_adj)
    in_weight_adj = by_rows(in_weight_adj, 3)

    pair_sums = jnp.zeros((2 * width,), f32)
    pair_sums = lax.dynamic_update_slice(pair_sums, sums[:part], (me * part,))
    pair_sums = lax.dynamic_update_slice(pair_sums, sums[2 * part :], (width + me * part,))
    vectors = [
        out_bias_adj,
        down_bias_adj,
        gain_one_adj,
        shift_one_adj,
        gain_two_adj,
        shift_two_adj,
        scale_one_adj,
        scale_two_adj,
    ]
    ups = jnp.zeros((group, units), f32)
    ups = lax.dynamic_update_slice(ups, up_bias_adj[None], (me, 0))
    packed = jnp.concatenate(
        [pair_sums.reshape(group, 2 * part), ups] + [v.reshape(group, part) for v in vectors], axis=1
    )
    count = packed.shape[1]
    packed = jnp.pad(packed, ((0, 0), (0, 2 * width - count))).reshape(group, 2, NX, 2 * width // 8)
    packed = reduce_rep(packed.transpose(1, 2, 0, 3), core, x)
    packed = lax.all_to_all(packed, SHARD, split_axis=0, concat_axis=0, tiled=True)
    packed = jnp.sum(packed.astype(f32), axis=0).astype(bf16)
    packed = spread_rep(packed).astype(f32)
    pair_sums = packed[: 2 * part]
    ups = packed[2 * part : 2 * part + units]
    at = 2 * part + units
    vectors = [packed[at + j * part : at + (j + 1) * part] for j in range(8)]

    return (
        layer_output[None],
        tokens_adjoint[None],
        in_weight_adj,
        pair_sums,
        out_weight_adj,
        vectors[0],
        up_weight_adj,
        ups,
        down_weight_adj,
        vectors[1],
        *vectors[2:],
    )


def solution(mesh):
    fine = Mesh(mesh.devices.reshape(2, NX, 2, NZ, 2), REP + SHARD)
    rows = P(REP, SHARD, None)
    matrix, vector = P(SHARD, None), P(SHARD)
    placed = (
        rows,
        matrix,
        vector,
        matrix,
        vector,
        matrix,
        vector,
        matrix,
        *[vector] * 7,
        rows,
    )
    return jax.shard_map(
        shards,
        mesh=fine,
        in_specs=placed,
        out_specs=(
            rows,
            rows,
            matrix,
            vector,
            matrix,
            vector,
            matrix,
            vector,
            matrix,
            *[vector] * 7,
        ),
        check_vma=False,
    )
```

time: 1480 us -> 472 us (0.32)
  waiting for transfers between devices: 1120 us -> 77.7 us
  starting transfers between devices: 0.73 us -> 146 us
  blocking collectives: 215 us -> 71.7 us
  local copies, waits for them, and re-layouts: 23.8 us -> 67.2 us
  matrix products: 83.5 us -> 46.4 us
  other arithmetic: 22.6 us -> 38.5 us
    reduce_scatter x4 -> x0, waiting for transfers between devices: 525 us -> none  [the longest x1 172 us: by_rows_layer(): lax.psum_scatter(current[6].astype(jnp.bfloat16), 'shard', scatter_dimens...]
    all_gather x6 -> x2, waiting for transfers between devices: 471 us -> 0.01 us  [spread_rep(): return lax.all_gather(block, ('core', 'x'), axis=0, tiled=True)]
    ppermute x0 -> x81, starting transfers between devices: none -> 124 us  [the longest x24 45.2 us: from_ahead(): return lax.ppermute(block, axis, [((i + k) % n, i) for i in range(n)])]
    all_gather x10 -> x3, blocking collectives: 145 us -> 71.7 us  [spread_rep(): return lax.all_gather(block, ('core', 'x'), axis=0, tiled=True)]
    unnamed x13 -> x2, waiting for transfers between devices: 73.8 us -> 0.03 us
    ppermute x0 -> x81, waiting for transfers between devices: none -> 70 us  [the longest x39 36.3 us: to_ahead(): return lax.ppermute(block, axis, [(i, (i + k) % n) for i in range(n)])]
    psum x1 -> x0, waiting for transfers between devices: 47.7 us -> none  [shards(): lax.psum(owned[0].astype(jnp.bfloat16), 'rep').astype(jnp.float32)]
    psum x1 -> x0, blocking collectives: 43.8 us -> none  [shards(): lax.psum(owned[1].astype(jnp.bfloat16), 'rep').astype(jnp.float32)]
  transfers between devices with their start and end apart: 12 -> 88, of which waited for: 11 -> 29; matrix products, arithmetic and copies ran while one was open for 5% -> 27% of each run, Pallas kernels for 0% -> 0%
where the time goes in v1:
time: 472 us; the launch traced here: 463 us
  starting transfers between devices  146 us (31%)
  waiting for transfers between devices  77.7 us (16%)
  blocking collectives  71.7 us (15%)
  local copies, waits for them, and re-layouts  67.2 us (14%)
  matrix products  46.4 us (10%)
  other arithmetic  38.5 us (8%)
  between operations  15.7 us (3%)
    all_gather x3, blocking collectives, spread_rep(): return lax.all_gather(block, ('core', 'x'), axis=0, tiled=True)  71.7 us
    unnamed x160, local copies, waits for them, and re-layouts  46.1 us
    ppermute x24, starting transfers between devices, from_ahead(): return lax.ppermute(block, axis, [((i + k) % n, i) for i in range(n)])  45.2 us
    ppermute x39, starting transfers between devices, to_ahead(): return lax.ppermute(block, axis, [(i, (i + k) % n) for i in range(n)])  38.3 us
    ppermute x39, waiting for transfers between devices, to_ahead(): return lax.ppermute(block, axis, [(i, (i + k) % n) for i in range(n)])  36.3 us
    ppermute x24, waiting for transfers between devices, from_ahead(): return lax.ppermute(block, axis, [((i + k) % n, i) for i in range(n)])  29.3 us
    ppermute x5, starting transfers between devices, reduce_rep(): lax.ppermute(pick(parts, 1 - core), 'core', SWAP).astype(f32)  18.7 us
    ppermute x5, starting transfers between devices, reduce_rep(): other = lax.ppermute(mine, 'yh', SWAP)  12.6 us
  transfers between devices with their start and end apart: 88, of which 29 were waited for; matrix products, arithmetic and copies ran while one was open for 27% of the time, Pallas kernels for 0%

profile of v1, /device:TPU:1, one launch (start us, length us, event | category | flops | bytes accessed | tf_op | source)
XLA Modules:
  0.0 463.3 jit_solution(16337567596292650824)
XLA Ops:
  7.2 2.5 collective-permute-start.30
  9.7 3.3 collective-permute-start.29
  27.5 4.2 all-to-all-start
  33.5 2.3 copy.77
  35.8 2.6 collective-permute-start
  40.4 8.2 %collective-permute-done = bf16[136,1024]{1,0:T(8,128)(2,1)S(1)} collective-permute-done((bf16[136,1024]{1,0:T(8,128)(2,1)}, bf16[136,1024]{1,0:T(8,128)(2,1)S(1)}, u32[]{:S(2)}, u32[]{:S(2)}) %collective-permute-start) | collective-permute-done | bytes 278560 | tf_op jit(solution)/shard_map/ppermute | solution.py:46
  50.4 3.3 collective-permute-start.5
  56.5 3.1 collective-permute-start.4
  62.7 3.5 collective-permute-done.4
  71.3 2.1 fusion.6
  73.5 7.2 %all-to-all-start.1 = ((bf16[128,8,512]{0,2,1:T(8,128)(2,1)}), bf16[128,8,512]{0,2,1:T(8,128)(2,1)}, u32[]{:S(2)}, u32[]{:S(2)}) async-start(bf16[128,8,512]{0,2,1:T(8,128)(2,1)} %bitcast.283), calls=%async_computation.1 | async-start | bytes 2097152 | tf_op jit(solution)/shard_map/all_to_all | solution.py:145
  82.6 2.9 add_convert_fusion.1
  92.8 2.7 collective-permute-start.12
  101.8 2.1 collective-permute-start.32
  105.6 2.7 collective-permute-start.9
  108.3 4.6 collective-permute-done.10
  113.0 4.3 collective-permute-done.32
  121.2 2.4 collective-permute-start.34
  128.7 6.8 %collective-permute-start.14 = (bf16[128,1024]{1,0:T(8,128)(2,1)}, bf16[128,1024]{1,0:T(8,128)(2,1)}, u32[]{:S(2)}, u32[]{:S(2)}) collective-permute-start(bf16[128,1024]{1,0:T(8,128)(2,1)} %get-tuple-element.35), channel_id=1, source_target_pairs={{2,0},{4,2},{6,4},{0,6},{3,1},{5,3},{7,5},{1,7},{10,8},{12,10},{14... | collective-permute-start | bytes 786440 | tf_op jit(solution)/shard_map/ppermute | solution.py:46
  136.3 2.3 copy.78
  140.2 2.1 collective-permute-start.20
  146.4 3.9 collective-permute-done.15
  153.4 6.1 %collective-permute-done.18 = bf16[128,1024]{1,0:T(8,128)(2,1)S(1)} collective-permute-done((bf16[128,1024]{1,0:T(8,128)(2,1)}, bf16[128,1024]{1,0:T(8,128)(2,1)S(1)}, u32[]{:S(2)}, u32[]{:S(2)}) %collective-permute-start.18) | collective-permute-done | bytes 262176 | tf_op jit(solution)/shard_map/ppermute | solution.py:46
  163.0 7.1 %multiply_convert_fusion.2 = (bf16[1024,512]{1,0:T(8,128)(2,1)S(1)}, f32[1024,512]{1,0:T(8,128)S(1)}, f32[1024,512]{1,0:T(8,128)S(1)}) fusion(f32[512]{0:T(512)S(1)} %convert_element_type.483, bf16[1024,1024]{1,0:T(8,128)(2,1)} %constant_dynamic-update-slice_fusion.1, bf16[1024,512]{1,0:T(8,128)(2,1)S(1)} %bitcast.302), kind=kOutput, calls=%fused_computation.23 | convolution fusion | flops 1108344832 | bytes 8390656 | tf_op jit(solution)/shard_map/dot_general | solution.py:31
  170.1 3.8 convert_reduce_fusion.1
  176.5 3.7 fusion.19
  186.1 2.1 collective-permute-start.26
  194.3 5.9 %collective-permute-done.38 = bf16[128,1024]{1,0:T(8,128)(2,1)S(1)} collective-permute-done((bf16[128,1024]{1,0:T(8,128)(2,1)S(1)}, bf16[128,1024]{1,0:T(8,128)(2,1)S(1)}, u32[]{:S(2)}, u32[]{:S(2)}) %collective-permute-start.38) | collective-permute-done | bytes 262176 | tf_op jit(solution)/shard_map/ppermute | solution.py:50
  205.0 5.6 %collective-permute-done.24 = bf16[128,1024]{1,0:T(8,128)(2,1)} collective-permute-done((bf16[128,1024]{1,0:T(8,128)(2,1)S(1)}, bf16[128,1024]{1,0:T(8,128)(2,1)}, u32[]{:S(2)}, u32[]{:S(2)}) %collective-permute-start.24) | collective-permute-done | bytes 262176 | tf_op jit(solution)/shard_map/ppermute | solution.py:50
  211.9 2.1 add_convert_fusion.6
  213.9 3.1 collective-permute-done.35
  218.6 2.3 collective-permute-done.36
  229.1 2.2 collective-permute-done.78
  231.4 2.7 collective-permute-start.80
  234.1 2.7 collective-permute-done.80
  242.9 2.7 collective-permute-start.74
  246.4 2.7 fusion.41
  251.3 2.9 collective-permute-start.75
  261.9 3.4 all-to-all-start.4
  267.2 4.2 all-to-all-done.4
  277.1 2.4 convolution_convert_fusion.6
  279.5 5.1 %convolution_convert_fusion.5 = bf16[2,64,1024]{2,1,0:T(8,128)(2,1)S(1)} fusion(bf16[1024,2,64]{0,2,1:T(8,128)(2,1)S(1)} %bitcast.285, f32[2,1024,1024]{1,2,0:T(8,128)} %copy-done.2, f32[2,1024]{1,0:T(2,128)S(1)} %log_add_fusion), kind=kOutput, calls=%fused_computation.50 | convolution fusion | flops 274857984 | bytes 8921088 | tf_op jit(solution)/shard_map/hqk,qhd->khd/dot_general | solution.py:109
  284.6 4.6 %multiply_reduce_fusion = (f32[2,1024]{1,0:T(2,128)S(1)}, f32[2,1024,1024]{1,2,0:T(8,128)S(1)}) fusion(f32[2,1024,1024]{1,2,0:T(8,128)} %copy-done.2, f32[2,1024]{1,0:T(2,128)S(1)} %log_add_fusion, bf16[1024,2,64]{0,2,1:T(8,128)(2,1)S(1)} %bitcast.286, bf16[1024,2,64]{0,2,1:T(8,128)(2,1)S(1)} %bitcast.288), kind=kOutput, calls=%fused_computation.1 | convolution fusion | flops 276822016 | bytes 17317888 | tf_op jit(solution)/shard_map/qhd,khd->hqk/dot_general | solution.py:104
  289.3 2.5 multiply_convert_fusion
  294.8 2.2 convolution_convert_fusion.4
  297.0 2.8 fusion.79
  300.4 13.2 %collective-permute-start.61 = (bf16[4,8,256]{2,1,0:T(8,128)(2,1)S(1)}, bf16[4,8,256]{2,1,0:T(8,128)(2,1)S(1)}, u32[]{:S(2)}, u32[]{:S(2)}) collective-permute-start(bf16[4,8,256]{2,1,0:T(8,128)(2,1)S(1)} %dynamic-slice_bitcast_fusion.15), channel_id=1, source_target_pairs={{0,8},{8,0},{1,9},{9,1},{2,10},{10,2},{3,11},{11,3},{4,12},{12,4},... | collective-permute-start | bytes 49160 | tf_op jit(solution)/shard_map/ppermute | solution.py:79
  313.6 2.0 fusion.20
  315.8 2.7 collective-permute-start.64
  322.4 2.8 collective-permute-start.65
  327.9 2.0 collective-permute-start.56
  331.7 3.3 all-to-all-start.3
  336.6 2.9 collective-permute-start.69
  342.1 13.9 %all-gather = bf16[8,1,256]{2,1,0:T(2,128)(2,1)S(1)} all-gather(bf16[1,1,256]{2,1,0:T(2,128)(2,1)S(1)} %reshape.339), channel_id=1, replica_groups=mesh['yh'=2,'x'=4,'core'=2,'z'=4,'yl'=2] {'core','x'}, dimensions={0}, use_global_device_ids=true | all-gather | bytes 4608 | tf_op jit(solution)/shard_map/all_gather | solution.py:89
  359.0 2.2 collective-permute-start.70
  363.7 2.7 collective-permute-start.51
  368.6 2.8 collective-permute-done.52
  375.1 31.8 %all_gather.17 = bf16[128,1024]{1,0:T(8,128)(2,1)S(1)} all-gather(bf16[16,1024]{1,0:T(8,128)(2,1)S(1)} %add_convert_fusion.12), channel_id=1, replica_groups=mesh['yh'=2,'x'=4,'core'=2,'z'=4,'yl'=2] {'core','x'}, dimensions={0}, use_global_device_ids=true | all-gather | bytes 294912 | tf_op jit(solution)/shard_map/all_gather | solution.py:89
  407.8 2.2 collective-permute-start.60
  414.2 3.4 all-to-all-start.2
  419.4 3.5 all-to-all-done.2
  423.0 26.0 %all_gather.15 = bf16[128,3072]{1,0:T(8,128)(2,1)S(1)} all-gather(bf16[16,3072]{1,0:T(8,128)(2,1)S(1)} %bitcast.315), channel_id=1, replica_groups=mesh['yh'=2,'x'=4,'core'=2,'z'=4,'yl'=2] {'core','x'}, dimensions={0}, use_global_device_ids=true | all-gather | bytes 884736 | tf_op jit(solution)/shard_map/all_gather | solution.py:89
  450.4 2.9 convert_element_type.612
  453.2 2.8 convert_element_type.596
  (401 shorter events, 161.1 us)
Async XLA Ops:
  7.2 94.6 %collective-permute-start.30 = (bf16[128,1024]{1,0:T(8,128)(2,1)}, bf16[128,1024]{1,0:T(8,128)(2,1)}, u32[]{:S(2)}, u32[]{:S(2)}) collective-permute-start(bf16[128,1024]{1,0:T(8,128)(2,1)} %bitcast.22), channel_id=1, source_target_pairs={{6,0},{0,2},{2,4},{4,6},{7,1},{1,3},{3,5},{5,7},{14,8},{8,10},{10,... | collective-permute-start | bytes 786440 | tf_op jit(solution)/shard_map/ppermute | solution.py:46
  9.7 85.8 %collective-permute-start.29 = (bf16[128,1024]{1,0:T(8,128)(2,1)}, bf16[128,1024]{1,0:T(8,128)(2,1)}, u32[]{:S(2)}, u32[]{:S(2)}) collective-permute-start(bf16[128,1024]{1,0:T(8,128)(2,1)} %bitcast.22), channel_id=1, source_target_pairs={{4,0},{6,2},{0,4},{2,6},{5,1},{7,3},{1,5},{3,7},{12,8},{14,10},{8,... | collective-permute-start | bytes 786440 | tf_op jit(solution)/shard_map/ppermute | solution.py:46
  13.0 83.0 %collective-permute-start.28 = (bf16[128,1024]{1,0:T(8,128)(2,1)}, bf16[128,1024]{1,0:T(8,128)(2,1)}, u32[]{:S(2)}, u32[]{:S(2)}) collective-permute-start(bf16[128,1024]{1,0:T(8,128)(2,1)} %bitcast.22), channel_id=1, source_target_pairs={{2,0},{4,2},{6,4},{0,6},{3,1},{5,3},{7,5},{1,7},{10,8},{12,10},{14... | collective-permute-start | bytes 786440 | tf_op jit(solution)/shard_map/ppermute | solution.py:46
  23.0 12.8 %collective-permute-start.3 = (bf16[136,1024]{1,0:T(8,128)(2,1)}, bf16[136,1024]{1,0:T(8,128)(2,1)}, u32[]{:S(2)}, u32[]{:S(2)}) collective-permute-start(bf16[136,1024]{1,0:T(8,128)(2,1)} %pad_maximum_fusion.1), channel_id=1, source_target_pairs={{0,1},{1,0},{2,3},{3,2},{4,5},{5,4},{6,7},{7,6},{8,9},{9,8},{10,11... | collective-permute-start | bytes 835592 | tf_op jit(solution)/shard_map/ppermute | solution.py:54
  24.3 14.8 %collective-permute-start.2 = (bf16[136,1024]{1,0:T(8,128)(2,1)}, bf16[136,1024]{1,0:T(8,128)(2,1)}, u32[]{:S(2)}, u32[]{:S(2)}) collective-permute-start(bf16[136,1024]{1,0:T(8,128)(2,1)} %pad_maximum_fusion.1), channel_id=1, source_target_pairs={{6,0},{0,2},{2,4},{4,6},{7,1},{1,3},{3,5},{5,7},{14,8},{8,10},{10,... | collective-permute-start | bytes 835592 | tf_op jit(solution)/shard_map/ppermute | solution.py:46
  27.5 46.0 %all-to-all-start = ((bf16[128,3,8,128]{0,3,1,2:T(8,128)(2,1)}), bf16[128,3,8,128]{0,3,1,2:T(8,128)(2,1)}, u32[]{:S(2)}, u32[]{:S(2)}) async-start(bf16[128,3,8,128]{0,3,1,2:T(8,128)(2,1)} %copy.74), calls=%async_computation | async-start | bytes 1572864 | tf_op jit(solution)/shard_map/all_to_all | solution.py:143
  35.8 12.8 %collective-permute-start = (bf16[136,1024]{1,0:T(8,128)(2,1)}, bf16[136,1024]{1,0:T(8,128)(2,1)S(1)}, u32[]{:S(2)}, u32[]{:S(2)}) collective-permute-start(bf16[136,1024]{1,0:T(8,128)(2,1)} %pad_maximum_fusion.1), channel_id=1, source_target_pairs={{2,0},{4,2},{6,4},{0,6},{3,1},{5,3},{7,5},{1,7},{10,8},{12,10},{14... | collective-permute-start | bytes 835592 | tf_op jit(solution)/shard_map/ppermute | solution.py:46
  39.1 11.3 %collective-permute-start.1 = (bf16[136,1024]{1,0:T(8,128)(2,1)}, bf16[136,1024]{1,0:T(8,128)(2,1)S(1)}, u32[]{:S(2)}, u32[]{:S(2)}) collective-permute-start(bf16[136,1024]{1,0:T(8,128)(2,1)} %pad_maximum_fusion.1), channel_id=1, source_target_pairs={{4,0},{6,2},{0,4},{2,6},{5,1},{7,3},{1,5},{3,7},{12,8},{14,10},{8,... | collective-permute-start | bytes 835592 | tf_op jit(solution)/shard_map/ppermute | solution.py:46
  50.4 10.4 %collective-permute-start.5 = (bf16[136,1024]{1,0:T(8,128)(2,1)}, bf16[136,1024]{1,0:T(8,128)(2,1)S(1)}, u32[]{:S(2)}, u32[]{:S(2)}) collective-permute-start(bf16[136,1024]{1,0:T(8,128)(2,1)} %collective-permute-done.3), channel_id=1, source_target_pairs={{4,0},{6,2},{0,4},{2,6},{5,1},{7,3},{1,5},{3,7},{12,8},{14,10},{8,... | collective-permute-start | bytes 835592 | tf_op jit(solution)/shard_map/ppermute | solution.py:46
  56.5 9.7 %collective-permute-start.4 = (bf16[136,1024]{1,0:T(8,128)(2,1)}, bf16[136,1024]{1,0:T(8,128)(2,1)S(1)}, u32[]{:S(2)}, u32[]{:S(2)}) collective-permute-start(bf16[136,1024]{1,0:T(8,128)(2,1)} %collective-permute-done.3), channel_id=1, source_target_pairs={{2,0},{4,2},{6,4},{0,6},{3,1},{5,3},{7,5},{1,7},{10,8},{12,10},{14... | collective-permute-start | bytes 835592 | tf_op jit(solution)/shard_map/ppermute | solution.py:46
  60.8 37.5 %collective-permute-start.31 = (bf16[128,1024]{1,0:T(8,128)(2,1)}, bf16[128,1024]{1,0:T(8,128)(2,1)}, u32[]{:S(2)}, u32[]{:S(2)}) collective-permute-start(bf16[128,1024]{1,0:T(8,128)(2,1)} %bitcast.22), channel_id=1, source_target_pairs={{0,1},{1,0},{2,3},{3,2},{4,5},{5,4},{6,7},{7,6},{8,9},{9,8},{10,11... | collective-permute-start | bytes 786440 | tf_op jit(solution)/shard_map/ppermute | solution.py:54
  73.5 62.8 %all-to-all-start.1 = ((bf16[128,8,512]{0,2,1:T(8,128)(2,1)}), bf16[128,8,512]{0,2,1:T(8,128)(2,1)}, u32[]{:S(2)}, u32[]{:S(2)}) async-start(bf16[128,8,512]{0,2,1:T(8,128)(2,1)} %bitcast.283), calls=%async_computation.1 | async-start | bytes 2097152 | tf_op jit(solution)/shard_map/all_to_all | solution.py:145
  80.7 369.7 %all-gather.6.cloned.1.call-start = ((), (), s32[]{:S(2)}) async-start(), calls=%async_computation.6 | async-start | bytes 1179648 | tf_op jit(solution)/shard_map/all_gather | solution.py:89
  92.8 12.8 %collective-permute-start.12 = (bf16[128,1024]{1,0:T(8,128)(2,1)S(1)}, bf16[128,1024]{1,0:T(8,128)(2,1)S(1)}, u32[]{:S(2)}, u32[]{:S(2)}) collective-permute-start(bf16[128,1024]{1,0:T(8,128)(2,1)S(1)} %get-tuple-element.59), channel_id=1, source_target_pairs={{0,6},{2,0},{4,2},{6,4},{1,7},{3,1},{5,3},{7,5},{8,14},{10,8},{12,... | collective-permute-start | bytes 786440 | tf_op jit(solution)/shard_map/ppermute | solution.py:50
  95.5 10.1 %collective-permute-start.11 = (bf16[128,1024]{1,0:T(8,128)(2,1)S(1)}, bf16[128,1024]{1,0:T(8,128)(2,1)S(1)}, u32[]{:S(2)}, u32[]{:S(2)}) collective-permute-start(bf16[128,1024]{1,0:T(8,128)(2,1)S(1)} %get-tuple-element.60), channel_id=1, source_target_pairs={{0,4},{2,6},{4,0},{6,2},{1,5},{3,7},{5,1},{7,3},{8,12},{10,14},{12... | collective-permute-start | bytes 786440 | tf_op jit(solution)/shard_map/ppermute | solution.py:50
  96.1 16.8 %collective-permute-start.10 = (bf16[128,1024]{1,0:T(8,128)(2,1)S(1)}, bf16[128,1024]{1,0:T(8,128)(2,1)S(1)}, u32[]{:S(2)}, u32[]{:S(2)}) collective-permute-start(bf16[128,1024]{1,0:T(8,128)(2,1)S(1)} %get-tuple-element.61), channel_id=1, source_target_pairs={{0,2},{2,4},{4,6},{6,0},{1,3},{3,5},{5,7},{7,1},{8,10},{10,12},{12... | collective-permute-start | bytes 786440 | tf_op jit(solution)/shard_map/ppermute | solution.py:50
  98.3 22.9 %collective-permute-start.33 = (bf16[128,1024]{1,0:T(8,128)(2,1)}, bf16[128,1024]{1,0:T(8,128)(2,1)S(1)}, u32[]{:S(2)}, u32[]{:S(2)}) collective-permute-start(bf16[128,1024]{1,0:T(8,128)(2,1)} %collective-permute-done.31), channel_id=1, source_target_pairs={{4,0},{6,2},{0,4},{2,6},{5,1},{7,3},{1,5},{3,7},{12,8},{14,10},{8,... | collective-permute-start | bytes 786440 | tf_op jit(solution)/shard_map/ppermute | solution.py:46
  101.8 15.5 %collective-permute-start.32 = (bf16[128,1024]{1,0:T(8,128)(2,1)}, bf16[128,1024]{1,0:T(8,128)(2,1)S(1)}, u32[]{:S(2)}, u32[]{:S(2)}) collective-permute-start(bf16[128,1024]{1,0:T(8,128)(2,1)} %collective-permute-done.31), channel_id=1, source_target_pairs={{2,0},{4,2},{6,4},{0,6},{3,1},{5,3},{7,5},{1,7},{10,8},{12,10},{14... | collective-permute-start | bytes 786440 | tf_op jit(solution)/shard_map/ppermute | solution.py:46
  105.6 18.8 %collective-permute-start.7 = (bf16[128,1024]{1,0:T(8,128)(2,1)S(1)}, bf16[128,1024]{1,0:T(8,128)(2,1)S(1)}, u32[]{:S(2)}, u32[]{:S(2)}) collective-permute-start(bf16[128,1024]{1,0:T(8,128)(2,1)S(1)} %get-tuple-element.58), channel_id=1, source_target_pairs={{0,2},{2,4},{4,6},{6,0},{1,3},{3,5},{5,7},{7,1},{8,10},{10,12},{12... | collective-permute-start | bytes 786440 | tf_op jit(solution)/shard_map/ppermute | solution.py:50
  105.6 19.3 %collective-permute-start.9 = (bf16[128,1024]{1,0:T(8,128)(2,1)S(1)}, bf16[128,1024]{1,0:T(8,128)(2,1)S(1)}, u32[]{:S(2)}, u32[]{:S(2)}) collective-permute-start(bf16[128,1024]{1,0:T(8,128)(2,1)S(1)} %get-tuple-element.62), channel_id=1, source_target_pairs={{0,6},{2,0},{4,2},{6,4},{1,7},{3,1},{5,3},{7,5},{8,14},{10,8},{12,... | collective-permute-start | bytes 786440 | tf_op jit(solution)/shard_map/ppermute | solution.py:50
  112.8 12.1 %collective-permute-start.8 = (bf16[128,1024]{1,0:T(8,128)(2,1)S(1)}, bf16[128,1024]{1,0:T(8,128)(2,1)S(1)}, u32[]{:S(2)}, u32[]{:S(2)}) collective-permute-start(bf16[128,1024]{1,0:T(8,128)(2,1)S(1)} %get-tuple-element.63), channel_id=1, source_target_pairs={{0,4},{2,6},{4,0},{6,2},{1,5},{3,7},{5,1},{7,3},{8,12},{10,14},{12... | collective-permute-start | bytes 786440 | tf_op jit(solution)/shard_map/ppermute | solution.py:50
  121.2 14.3 %collective-permute-start.34 = (bf16[128,1024]{1,0:T(8,128)(2,1)}, bf16[128,1024]{1,0:T(8,128)(2,1)S(1)}, u32[]{:S(2)}, u32[]{:S(2)}) collective-permute-start(bf16[128,1024]{1,0:T(8,128)(2,1)} %collective-permute-done.31), channel_id=1, source_target_pairs={{6,0},{0,2},{2,4},{4,6},{7,1},{1,3},{3,5},{5,7},{14,8},{8,10},{10,... | collective-permute-start | bytes 786440 | tf_op jit(solution)/shard_map/ppermute | solution.py:46
  127.1 13.1 %collective-permute-start.17 = (bf16[128,1024]{1,0:T(8,128)(2,1)}, bf16[128,1024]{1,0:T(8,128)(2,1)}, u32[]{:S(2)}, u32[]{:S(2)}) collective-permute-start(bf16[128,1024]{1,0:T(8,128)(2,1)} %get-tuple-element.35), channel_id=1, source_target_pairs={{0,1},{1,0},{2,3},{3,2},{4,5},{5,4},{6,7},{7,6},{8,9},{9,8},{10,11... | collective-permute-start | bytes 786440 | tf_op jit(solution)/shard_map/ppermute | solution.py:54
  128.7 14.2 %collective-permute-start.14 = (bf16[128,1024]{1,0:T(8,128)(2,1)}, bf16[128,1024]{1,0:T(8,128)(2,1)}, u32[]{:S(2)}, u32[]{:S(2)}) collective-permute-start(bf16[128,1024]{1,0:T(8,128)(2,1)} %get-tuple-element.35), channel_id=1, source_target_pairs={{2,0},{4,2},{6,4},{0,6},{3,1},{5,3},{7,5},{1,7},{10,8},{12,10},{14... | collective-permute-start | bytes 786440 | tf_op jit(solution)/shard_map/ppermute | solution.py:46
  138.5 12.5 %collective-permute-start.16 = (bf16[128,1024]{1,0:T(8,128)(2,1)}, bf16[128,1024]{1,0:T(8,128)(2,1)S(1)}, u32[]{:S(2)}, u32[]{:S(2)}) collective-permute-start(bf16[128,1024]{1,0:T(8,128)(2,1)} %get-tuple-element.35), channel_id=1, source_target_pairs={{6,0},{0,2},{2,4},{4,6},{7,1},{1,3},{3,5},{5,7},{14,8},{8,10},{10,... | collective-permute-start | bytes 786440 | tf_op jit(solution)/shard_map/ppermute | solution.py:46
  138.5 11.8 %collective-permute-start.15 = (bf16[128,1024]{1,0:T(8,128)(2,1)}, bf16[128,1024]{1,0:T(8,128)(2,1)S(1)}, u32[]{:S(2)}, u32[]{:S(2)}) collective-permute-start(bf16[128,1024]{1,0:T(8,128)(2,1)} %get-tuple-element.35), channel_id=1, source_target_pairs={{4,0},{6,2},{0,4},{2,6},{5,1},{7,3},{1,5},{3,7},{12,8},{14,10},{8,... | collective-permute-start | bytes 786440 | tf_op jit(solution)/shard_map/ppermute | solution.py:46
  140.2 22.1 %collective-permute-start.20 = (bf16[128,1024]{1,0:T(8,128)(2,1)}, bf16[128,1024]{1,0:T(8,128)(2,1)S(1)}, u32[]{:S(2)}, u32[]{:S(2)}) collective-permute-start(bf16[128,1024]{1,0:T(8,128)(2,1)} %collective-permute-done.17), channel_id=1, source_target_pairs={{6,0},{0,2},{2,4},{4,6},{7,1},{1,3},{3,5},{5,7},{14,8},{8,10},{10,... | collective-permute-start | bytes 786440 | tf_op jit(solution)/shard_map/ppermute | solution.py:46
  142.2 19.4 %collective-permute-start.19 = (bf16[128,1024]{1,0:T(8,128)(2,1)}, bf16[128,1024]{1,0:T(8,128)(2,1)S(1)}, u32[]{:S(2)}, u32[]{:S(2)}) collective-permute-start(bf16[128,1024]{1,0:T(8,128)(2,1)} %collective-permute-done.17), channel_id=1, source_target_pairs={{4,0},{6,2},{0,4},{2,6},{5,1},{7,3},{1,5},{3,7},{12,8},{14,10},{8,... | collective-permute-start | bytes 786440 | tf_op jit(solution)/shard_map/ppermute | solution.py:46
  142.9 16.6 %collective-permute-start.18 = (bf16[128,1024]{1,0:T(8,128)(2,1)}, bf16[128,1024]{1,0:T(8,128)(2,1)S(1)}, u32[]{:S(2)}, u32[]{:S(2)}) collective-permute-start(bf16[128,1024]{1,0:T(8,128)(2,1)} %collective-permute-done.17), channel_id=1, source_target_pairs={{2,0},{4,2},{6,4},{0,6},{3,1},{5,3},{7,5},{1,7},{10,8},{12,10},{14... | collective-permute-start | bytes 786440 | tf_op jit(solution)/shard_map/ppermute | solution.py:46
  184.5 15.6 %collective-permute-start.38 = (bf16[128,1024]{1,0:T(8,128)(2,1)S(1)}, bf16[128,1024]{1,0:T(8,128)(2,1)S(1)}, u32[]{:S(2)}, u32[]{:S(2)}) collective-permute-start(bf16[128,1024]{1,0:T(8,128)(2,1)S(1)} %get-tuple-element.49), channel_id=1, source_target_pairs={{0,2},{2,4},{4,6},{6,0},{1,3},{3,5},{5,7},{7,1},{8,10},{10,12},{12... | collective-permute-start | bytes 786440 | tf_op jit(solution)/shard_map/ppermute | solution.py:50
  186.1 16.8 %collective-permute-start.26 = (bf16[128,1024]{1,0:T(8,128)(2,1)S(1)}, bf16[128,1024]{1,0:T(8,128)(2,1)S(1)}, u32[]{:S(2)}, u32[]{:S(2)}) collective-permute-start(bf16[128,1024]{1,0:T(8,128)(2,1)S(1)} %get-tuple-element.53), channel_id=1, source_target_pairs={{0,6},{2,0},{4,2},{6,4},{1,7},{3,1},{5,3},{7,5},{8,14},{10,8},{12,... | collective-permute-start | bytes 786440 | tf_op jit(solution)/shard_map/ppermute | solution.py:50
  188.2 15.8 %collective-permute-start.25 = (bf16[128,1024]{1,0:T(8,128)(2,1)S(1)}, bf16[128,1024]{1,0:T(8,128)(2,1)S(1)}, u32[]{:S(2)}, u32[]{:S(2)}) collective-permute-start(bf16[128,1024]{1,0:T(8,128)(2,1)S(1)} %get-tuple-element.54), channel_id=1, source_target_pairs={{0,4},{2,6},{4,0},{6,2},{1,5},{3,7},{5,1},{7,3},{8,12},{10,14},{12... | collective-permute-start | bytes 786440 | tf_op jit(solution)/shard_map/ppermute | solution.py:50
  191.7 18.9 %collective-permute-start.24 = (bf16[128,1024]{1,0:T(8,128)(2,1)S(1)}, bf16[128,1024]{1,0:T(8,128)(2,1)}, u32[]{:S(2)}, u32[]{:S(2)}) collective-permute-start(bf16[128,1024]{1,0:T(8,128)(2,1)S(1)} %get-tuple-element.55), channel_id=1, source_target_pairs={{0,2},{2,4},{4,6},{6,0},{1,3},{3,5},{5,7},{7,1},{8,10},{10,12},{12... | collective-permute-start | bytes 786440 | tf_op jit(solution)/shard_map/ppermute | solution.py:50
  192.7 24.4 %collective-permute-start.35 = (bf16[128,1024]{1,0:T(8,128)(2,1)}, bf16[128,1024]{1,0:T(8,128)(2,1)}, u32[]{:S(2)}, u32[]{:S(2)}) collective-permute-start(bf16[128,1024]{1,0:T(8,128)(2,1)} %get-tuple-element.46), channel_id=1, source_target_pairs={{0,2},{2,4},{4,6},{6,0},{1,3},{3,5},{5,7},{7,1},{8,10},{10,12},{12... | collective-permute-start | bytes 786440 | tf_op jit(solution)/shard_map/ppermute | solution.py:50
  200.2 18.2 %collective-permute-start.37 = (bf16[128,1024]{1,0:T(8,128)(2,1)}, bf16[128,1024]{1,0:T(8,128)(2,1)}, u32[]{:S(2)}, u32[]{:S(2)}) collective-permute-start(bf16[128,1024]{1,0:T(8,128)(2,1)} %get-tuple-element.50), channel_id=1, source_target_pairs={{0,6},{2,0},{4,2},{6,4},{1,7},{3,1},{5,3},{7,5},{8,14},{10,8},{12,... | collective-permute-start | bytes 786440 | tf_op jit(solution)/shard_map/ppermute | solution.py:50
  202.9 18.0 %collective-permute-start.36 = (bf16[128,1024]{1,0:T(8,128)(2,1)}, bf16[128,1024]{1,0:T(8,128)(2,1)}, u32[]{:S(2)}, u32[]{:S(2)}) collective-permute-start(bf16[128,1024]{1,0:T(8,128)(2,1)} %get-tuple-element.51), channel_id=1, source_target_pairs={{0,4},{2,6},{4,0},{6,2},{1,5},{3,7},{5,1},{7,3},{8,12},{10,14},{12... | collective-permute-start | bytes 786440 | tf_op jit(solution)/shard_map/ppermute | solution.py:50
  204.0 17.0 %collective-permute-start.41 = (bf16[128,1024]{1,0:T(8,128)(2,1)}, bf16[128,1024]{1,0:T(8,128)(2,1)}, u32[]{:S(2)}, u32[]{:S(2)}) collective-permute-start(bf16[128,1024]{1,0:T(8,128)(2,1)} %add_convert_fusion.4), channel_id=1, source_target_pairs={{0,1},{1,0},{2,3},{3,2},{4,5},{5,4},{6,7},{7,6},{8,9},{9,8},{10,11... | collective-permute-start | bytes 786440 | tf_op jit(solution)/shard_map/ppermute | solution.py:68
  210.6 12.0 %collective-permute-start.76 = (bf16[4,64,1024]{2,1,0:T(8,128)(2,1)}, bf16[4,64,1024]{2,1,0:T(8,128)(2,1)S(1)}, u32[]{:S(2)}, u32[]{:S(2)}) collective-permute-start(bf16[4,64,1024]{2,1,0:T(8,128)(2,1)} %dynamic-slice_bitcast_fusion), channel_id=1, source_target_pairs={{0,8},{8,0},{1,9},{9,1},{2,10},{10,2},{3,11},{11,3},{4,12},{12,4},... | collective-permute-start | bytes 1572872 | tf_op jit(solution)/shard_map/ppermute | solution.py:79
  217.1 21.8 %collective-permute-start.71 = (bf16[4,8,16,512]{3,2,0,1:T(8,128)(2,1)}, bf16[4,8,16,512]{3,2,0,1:T(8,128)(2,1)}, u32[]{:S(2)}, u32[]{:S(2)}) collective-permute-start(bf16[4,8,16,512]{3,2,0,1:T(8,128)(2,1)} %dynamic-slice_bitcast_fusion.1), channel_id=1, source_target_pairs={{0,8},{8,0},{1,9},{9,1},{2,10},{10,2},{3,11},{11,3},{4,12},{12,4},... | collective-permute-start | bytes 1572872 | tf_op jit(solution)/shard_map/ppermute | solution.py:79
  218.4 23.4 %collective-permute-start.21 = (bf16[128,1024]{1,0:T(8,128)(2,1)}, bf16[128,1024]{1,0:T(8,128)(2,1)}, u32[]{:S(2)}, u32[]{:S(2)}) collective-permute-start(bf16[128,1024]{1,0:T(8,128)(2,1)} %get-tuple-element.52), channel_id=1, source_target_pairs={{0,2},{2,4},{4,6},{6,0},{1,3},{3,5},{5,7},{7,1},{8,10},{10,12},{12... | collective-permute-start | bytes 786440 | tf_op jit(solution)/shard_map/ppermute | solution.py:50
  228.4 14.6 %collective-permute-start.23 = (bf16[128,1024]{1,0:T(8,128)(2,1)}, bf16[128,1024]{1,0:T(8,128)(2,1)}, u32[]{:S(2)}, u32[]{:S(2)}) collective-permute-start(bf16[128,1024]{1,0:T(8,128)(2,1)} %get-tuple-element.56), channel_id=1, source_target_pairs={{0,6},{2,0},{4,2},{6,4},{1,7},{3,1},{5,3},{7,5},{8,14},{10,8},{12,... | collective-permute-start | bytes 786440 | tf_op jit(solution)/shard_map/ppermute | solution.py:50
  228.4 14.6 %collective-permute-start.22 = (bf16[128,1024]{1,0:T(8,128)(2,1)}, bf16[128,1024]{1,0:T(8,128)(2,1)}, u32[]{:S(2)}, u32[]{:S(2)}) collective-permute-start(bf16[128,1024]{1,0:T(8,128)(2,1)} %get-tuple-element.57), channel_id=1, source_target_pairs={{0,4},{2,6},{4,0},{6,2},{1,5},{3,7},{5,1},{7,3},{8,12},{10,14},{12... | collective-permute-start | bytes 786440 | tf_op jit(solution)/shard_map/ppermute | solution.py:50
  238.9 15.2 %collective-permute-start.45 = (bf16[128,1024]{1,0:T(8,128)(2,1)S(1)}, bf16[128,1024]{1,0:T(8,128)(2,1)}, u32[]{:S(2)}, u32[]{:S(2)}) collective-permute-start(bf16[128,1024]{1,0:T(8,128)(2,1)S(1)} %get-tuple-element.26), channel_id=1, source_target_pairs={{0,1},{1,0},{2,3},{3,2},{4,5},{5,4},{6,7},{7,6},{8,9},{9,8},{10,11... | collective-permute-start | bytes 786440 | tf_op jit(solution)/shard_map/ppermute | solution.py:54
  241.8 14.0 %collective-permute-start.42 = (bf16[128,1024]{1,0:T(8,128)(2,1)S(1)}, bf16[128,1024]{1,0:T(8,128)(2,1)S(1)}, u32[]{:S(2)}, u32[]{:S(2)}) collective-permute-start(bf16[128,1024]{1,0:T(8,128)(2,1)S(1)} %get-tuple-element.26), channel_id=1, source_target_pairs={{2,0},{4,2},{6,4},{0,6},{3,1},{5,3},{7,5},{1,7},{10,8},{12,10},{14... | collective-permute-start | bytes 786440 | tf_op jit(solution)/shard_map/ppermute | solution.py:46
  249.8 10.7 %collective-permute-start.44 = (bf16[128,1024]{1,0:T(8,128)(2,1)S(1)}, bf16[128,1024]{1,0:T(8,128)(2,1)S(1)}, u32[]{:S(2)}, u32[]{:S(2)}) collective-permute-start(bf16[128,1024]{1,0:T(8,128)(2,1)S(1)} %get-tuple-element.26), channel_id=1, source_target_pairs={{6,0},{0,2},{2,4},{4,6},{7,1},{1,3},{3,5},{5,7},{14,8},{8,10},{10,... | collective-permute-start | bytes 786440 | tf_op jit(solution)/shard_map/ppermute | solution.py:46
  251.3 9.9 %collective-permute-start.75 = (bf16[8,16,512]{2,1,0:T(8,128)(2,1)S(1)}, bf16[8,16,512]{2,1,0:T(8,128)(2,1)S(1)}, u32[]{:S(2)}, u32[]{:S(2)}) collective-permute-start(bf16[8,16,512]{2,1,0:T(8,128)(2,1)S(1)} %fusion.50), channel_id=1, source_target_pairs={{0,64},{64,0},{1,65},{65,1},{2,66},{66,2},{3,67},{67,3},{4,68},{68... | collective-permute-start | bytes 393224 | tf_op jit(solution)/shard_map/ppermute | solution.py:84
  254.1 21.3 %collective-permute-start.48 = (bf16[128,1024]{1,0:T(8,128)(2,1)}, bf16[128,1024]{1,0:T(8,128)(2,1)}, u32[]{:S(2)}, u32[]{:S(2)}) collective-permute-start(bf16[128,1024]{1,0:T(8,128)(2,1)} %collective-permute-done.45), channel_id=1, source_target_pairs={{6,0},{0,2},{2,4},{4,6},{7,1},{1,3},{3,5},{5,7},{14,8},{8,10},{10,... | collective-permute-start | bytes 786440 | tf_op jit(solution)/shard_map/ppermute | solution.py:46
  255.8 17.9 %collective-permute-start.47 = (bf16[128,1024]{1,0:T(8,128)(2,1)}, bf16[128,1024]{1,0:T(8,128)(2,1)}, u32[]{:S(2)}, u32[]{:S(2)}) collective-permute-start(bf16[128,1024]{1,0:T(8,128)(2,1)} %collective-permute-done.45), channel_id=1, source_target_pairs={{4,0},{6,2},{0,4},{2,6},{5,1},{7,3},{1,5},{3,7},{12,8},{14,10},{8,... | collective-permute-start | bytes 786440 | tf_op jit(solution)/shard_map/ppermute | solution.py:46
  258.3 13.7 %collective-permute-start.46 = (bf16[128,1024]{1,0:T(8,128)(2,1)}, bf16[128,1024]{1,0:T(8,128)(2,1)}, u32[]{:S(2)}, u32[]{:S(2)}) collective-permute-start(bf16[128,1024]{1,0:T(8,128)(2,1)} %collective-permute-done.45), channel_id=1, source_target_pairs={{2,0},{4,2},{6,4},{0,6},{3,1},{5,3},{7,5},{1,7},{10,8},{12,10},{14... | collective-permute-start | bytes 786440 | tf_op jit(solution)/shard_map/ppermute | solution.py:46
  265.2 188.0 %all-gather.4.cloned.1.call-start = ((), (), s32[]{:S(2)}) async-start(), calls=%async_computation.5 | async-start | bytes 1179648 | tf_op jit(solution)/shard_map/all_gather | solution.py:89
  300.4 15.3 %collective-permute-start.61 = (bf16[4,8,256]{2,1,0:T(8,128)(2,1)S(1)}, bf16[4,8,256]{2,1,0:T(8,128)(2,1)S(1)}, u32[]{:S(2)}, u32[]{:S(2)}) collective-permute-start(bf16[4,8,256]{2,1,0:T(8,128)(2,1)S(1)} %dynamic-slice_bitcast_fusion.15), channel_id=1, source_target_pairs={{0,8},{8,0},{1,9},{9,1},{2,10},{10,2},{3,11},{11,3},{4,12},{12,4},... | collective-permute-start | bytes 49160 | tf_op jit(solution)/shard_map/ppermute | solution.py:79
  320.0 15.0 %collective-permute-start.66 = (bf16[4,16,1024]{2,1,0:T(8,128)(2,1)}, bf16[4,16,1024]{2,1,0:T(8,128)(2,1)S(1)}, u32[]{:S(2)}, u32[]{:S(2)}) collective-permute-start(bf16[4,16,1024]{2,1,0:T(8,128)(2,1)} %dynamic-slice_bitcast_fusion.8), channel_id=1, source_target_pairs={{0,8},{8,0},{1,9},{9,1},{2,10},{10,2},{3,11},{11,3},{4,12},{12,4},... | collective-permute-start | bytes 393224 | tf_op jit(solution)/shard_map/ppermute | solution.py:79
  327.9 35.8 %collective-permute-start.56 = (bf16[4,8,16,384]{3,2,1,0:T(8,128)(2,1)}, bf16[4,8,16,384]{3,2,1,0:T(8,128)(2,1)}, u32[]{:S(2)}, u32[]{:S(2)}) collective-permute-start(bf16[4,8,16,384]{3,2,1,0:T(8,128)(2,1)} %bitcast.276), channel_id=1, source_target_pairs={{0,8},{8,0},{1,9},{9,1},{2,10},{10,2},{3,11},{11,3},{4,12},{12,4},... | collective-permute-start | bytes 1179656 | tf_op jit(solution)/shard_map/ppermute | solution.py:79
  331.7 10.3 %all-to-all-start.3 = ((bf16[8,2,128]{2,1,0:T(2,128)(2,1)}), bf16[8,2,128]{2,1,0:T(2,128)(2,1)S(1)}, u32[]{:S(2)}, u32[]{:S(2)}) async-start(bf16[8,2,128]{2,1,0:T(2,128)(2,1)} %reshape.345), calls=%async_computation.3 | async-start | bytes 8192 | tf_op jit(solution)/shard_map/all_to_all | solution.py:279
  336.6 19.4 %collective-permute-start.67 = (bf16[16,1024]{1,0:T(8,128)(2,1)}, bf16[16,1024]{1,0:T(8,128)(2,1)S(1)}, u32[]{:S(2)}, u32[]{:S(2)}) collective-permute-start(bf16[16,1024]{1,0:T(8,128)(2,1)} %get-tuple-element.80), channel_id=1, source_target_pairs={{0,16},{16,32},{32,48},{48,0},{1,17},{17,33},{33,49},{49,1},{2,18}... | collective-permute-start | bytes 98312 | tf_op jit(solution)/shard_map/ppermute | solution.py:50
  336.6 20.4 %collective-permute-start.69 = (bf16[16,1024]{1,0:T(8,128)(2,1)}, bf16[16,1024]{1,0:T(8,128)(2,1)S(1)}, u32[]{:S(2)}, u32[]{:S(2)}) collective-permute-start(bf16[16,1024]{1,0:T(8,128)(2,1)} %get-tuple-element.81), channel_id=1, source_target_pairs={{0,48},{16,0},{32,16},{48,32},{1,49},{17,1},{33,17},{49,33},{2,50}... | collective-permute-start | bytes 98312 | tf_op jit(solution)/shard_map/ppermute | solution.py:50
  339.5 19.5 %collective-permute-start.68 = (bf16[16,1024]{1,0:T(8,128)(2,1)}, bf16[16,1024]{1,0:T(8,128)(2,1)S(1)}, u32[]{:S(2)}, u32[]{:S(2)}) collective-permute-start(bf16[16,1024]{1,0:T(8,128)(2,1)} %get-tuple-element.82), channel_id=1, source_target_pairs={{0,32},{16,48},{32,0},{48,16},{1,33},{17,49},{33,1},{49,17},{2,34}... | collective-permute-start | bytes 98312 | tf_op jit(solution)/shard_map/ppermute | solution.py:50
  340.7 69.3 %collective-permute-start.49 = (bf16[128,1024]{1,0:T(8,128)(2,1)}, bf16[128,1024]{1,0:T(8,128)(2,1)}, u32[]{:S(2)}, u32[]{:S(2)}) collective-permute-start(bf16[128,1024]{1,0:T(8,128)(2,1)} %get-tuple-element.40), channel_id=1, source_target_pairs={{0,2},{2,4},{4,6},{6,0},{1,3},{3,5},{5,7},{7,1},{8,10},{10,12},{12... | collective-permute-start | bytes 786440 | tf_op jit(solution)/shard_map/ppermute | solution.py:50
  356.0 11.6 %collective-permute-start.54 = (bf16[128,1024]{1,0:T(8,128)(2,1)}, bf16[128,1024]{1,0:T(8,128)(2,1)S(1)}, u32[]{:S(2)}, u32[]{:S(2)}) collective-permute-start(bf16[128,1024]{1,0:T(8,128)(2,1)} %get-tuple-element.41), channel_id=1, source_target_pairs={{0,6},{2,0},{4,2},{6,4},{1,7},{3,1},{5,3},{7,5},{8,14},{10,8},{12,... | collective-permute-start | bytes 786440 | tf_op jit(solution)/shard_map/ppermute | solution.py:50
  357.0 10.7 %collective-permute-start.53 = (bf16[128,1024]{1,0:T(8,128)(2,1)}, bf16[128,1024]{1,0:T(8,128)(2,1)S(1)}, u32[]{:S(2)}, u32[]{:S(2)}) collective-permute-start(bf16[128,1024]{1,0:T(8,128)(2,1)} %get-tuple-element.42), channel_id=1, source_target_pairs={{0,4},{2,6},{4,0},{6,2},{1,5},{3,7},{5,1},{7,3},{8,12},{10,14},{12... | collective-permute-start | bytes 786440 | tf_op jit(solution)/shard_map/ppermute | solution.py:50
  363.7 46.3 %collective-permute-start.51 = (bf16[128,1024]{1,0:T(8,128)(2,1)}, bf16[128,1024]{1,0:T(8,128)(2,1)S(1)}, u32[]{:S(2)}, u32[]{:S(2)}) collective-permute-start(bf16[128,1024]{1,0:T(8,128)(2,1)} %get-tuple-element.44), channel_id=1, source_target_pairs={{0,6},{2,0},{4,2},{6,4},{1,7},{3,1},{5,3},{7,5},{8,14},{10,8},{12,... | collective-permute-start | bytes 786440 | tf_op jit(solution)/shard_map/ppermute | solution.py:50
  367.6 42.4 %collective-permute-start.50 = (bf16[128,1024]{1,0:T(8,128)(2,1)}, bf16[128,1024]{1,0:T(8,128)(2,1)S(1)}, u32[]{:S(2)}, u32[]{:S(2)}) collective-permute-start(bf16[128,1024]{1,0:T(8,128)(2,1)} %get-tuple-element.45), channel_id=1, source_target_pairs={{0,4},{2,6},{4,0},{6,2},{1,5},{3,7},{5,1},{7,3},{8,12},{10,14},{12... | collective-permute-start | bytes 786440 | tf_op jit(solution)/shard_map/ppermute | solution.py:50
  372.7 37.3 %collective-permute-start.55 = (bf16[128,1024]{1,0:T(8,128)(2,1)S(1)}, bf16[128,1024]{1,0:T(8,128)(2,1)S(1)}, u32[]{:S(2)}, u32[]{:S(2)}) collective-permute-start(bf16[128,1024]{1,0:T(8,128)(2,1)S(1)} %add_convert_fusion.3), channel_id=1, source_target_pairs={{0,1},{1,0},{2,3},{3,2},{4,5},{5,4},{6,7},{7,6},{8,9},{9,8},{10,11... | collective-permute-start | bytes 786440 | tf_op jit(solution)/shard_map/ppermute | solution.py:68
  375.1 32.6 %collective-permute-start.58 = (bf16[8,16,384]{2,1,0:T(8,128)(2,1)S(1)}, bf16[8,16,384]{2,1,0:T(8,128)(2,1)S(1)}, u32[]{:S(2)}, u32[]{:S(2)}) collective-permute-start(bf16[8,16,384]{2,1,0:T(8,128)(2,1)S(1)} %get-tuple-element.77), channel_id=1, source_target_pairs={{0,32},{16,48},{32,0},{48,16},{1,33},{17,49},{33,1},{49,17},{2,34}... | collective-permute-start | bytes 294920 | tf_op jit(solution)/shard_map/ppermute | solution.py:50
  (70 other events, 729.2 us)
Sparse Core Ops, SparseCore 0:
  237.7 29.4 all-gather.5
  272.1 33.9 all-gather.3
